TPU v7x, 256 devices: a whole 4x4x8 slice. The times are simulated.
256 devices in a mesh: orient: 32 (over z, x), dom: 2 (over core), shell: 4 (over y).
Axes of the slice: x: 4, y: 4, z: 8, core: 2. Of those that a mesh axis runs over, the one named last changes fastest.
Arguments:
- references: bfloat16 [16384, 2, 4096], P('orient', None, 'shell'), may hold values from -6 to 6
- images: bfloat16 [4096, 2, 4096], P(('orient', 'dom'), None, 'shell'), may hold values from -20 to 20
- noise_var: float32 [64], replicated, may hold values from 32 to 128
- shell_of: int32 [4096], P('shell'), may hold values from 0 to 63, never falling along the last dimension, each value on 1 to 128 neighbouring positions
- kept_blocks: int32 [32, 2, 24], P('orient', 'dom'), may hold values from -1 to 31, as said below
Outputs:
- weighted: float32 [16384, 2, 4096], P(('orient', 'dom'), None, 'shell')
- log_norm: float32 [4096], P(('orient', 'dom'))
Inputs may be any that keep to these rules, and one draw needn't show every extreme that they name: `kept_blocks`: each list holds distinct block numbers first, then -1 entries; the list of orientation block o and group d always starts with o; some list holds 24 blocks.
All inputs are finite; a program needn't handle non-finite values.
Results may differ from a plain program's by a relative error of at most 0.0051.
Values may be sent and summed in bfloat16 or wider, within the bound.
No kernel may reach another device: no remote copies, remote signals or barrier semaphores. Data moves between devices by JAX's collectives and lax.ppermute only.
A program may use at most 64 MiB of HBM per device.

v0:
```python
import jax
import jax.numpy as jnp
from jax import lax
from jax.experimental import pallas as pl
from jax.experimental.pallas import tpu as pltpu
from jax.sharding import Mesh
from jax.sharding import PartitionSpec as P

floor_value = -1e30

NZ, NX, NY = 8, 4, 4
BLOCKS = NZ * NX
ROWS = 64
HALF = 32
MOST = 24
REFS = 512
COLS = 2048
QUARTER = MOST * 8

ORDER_A = [[(dz, dx) for dx in range(4)] for dz in (0, 7, 1, 6, 2, 5, 3)] + [
    [(4, 0), (4, 1)],
    [(4, 2), (4, 3)],
]
ORDER_B = [[(dz, dx) for dz in range(8)] for dx in (0, 3, 1)] + [
    [(dz, 2) for dz in range(4)],
    [(dz, 2) for dz in range(4, 8)],
]
VMEM = pl.BlockSpec(memory_space=pltpu.VMEM)
SMEM = pl.BlockSpec(memory_space=pltpu.SMEM)
ANY = pl.BlockSpec(memory_space=pl.ANY)


def step(value, axis, count, by):
    return lax.ppermute(value, axis, [(i, (i + by) % count) for i in range(count)])


def fetch(arrays, whole, sems, first=0):
    copies, base = [], 0
    for i, piece in enumerate(arrays):
        rows = piece.shape[0]
        copy = pltpu.make_async_copy(
            piece, whole.at[pl.ds(base, rows), :], sems.at[first + i]
        )
        copy.start()
        copies.append((copy, base, rows))
        base += rows
    return copies


def join_kernel(*rest):
    arrays, (out, sems) = rest[:-2], rest[-2:]
    for copy, _, _ in fetch(arrays, out, sems):
        copy.wait()


def joined(arrays):
    rows = sum(a.shape[0] for a in arrays)
    return pl.pallas_call(
        join_kernel,
        out_shape=jax.ShapeDtypeStruct((rows, COLS), jnp.bfloat16),
        in_specs=[ANY] * len(arrays),
        out_specs=ANY,
        scratch_shapes=[pltpu.SemaphoreType.DMA((len(arrays),))],
        compiler_params=pltpu.CompilerParams(vmem_limit_bytes=4 << 20),
        cost_estimate=pl.CostEstimate(
            flops=0, bytes_accessed=2 * rows * COLS, transcendentals=0
        ),
        name="joined",
    )(*arrays)


def halves_kernel(first, second, top, low):
    rows = top.shape[0]
    top[...] = first[:rows, :]
    low[...] = second[rows:, :]


def halves(first, second):
    rows, wide = first.shape
    half = jax.ShapeDtypeStruct((rows // 2, wide), first.dtype)
    return pl.pallas_call(
        halves_kernel,
        out_shape=(half, half),
        in_specs=[VMEM] * 2,
        out_specs=(VMEM, VMEM),
        compiler_params=pltpu.CompilerParams(vmem_limit_bytes=4 << 20),
        name="halves",
    )(first, second)


def both_ways(up, down, axis, count):
    return step(up, axis, count, 1), step(down, axis, count, -1)


def gather(half_a, half_b, flat, norm_of, tab):
    downs, ups = [half_b], [half_b]
    down, up = both_ways(half_b, half_b, "z", NZ)
    low, high = both_ways(half_a, half_a, "x", NX)
    across = step(half_a, "x", NX, 2)
    downs.append(down)
    ups.append(up)
    for _ in range(2):
        down, up = both_ways(downs[-1], ups[-1], "z", NZ)
        downs.append(down)
        ups.append(up)
    far = step(downs[-1], "z", NZ, 1)
    mine_a = joined([half_a, high, across, low])
    mine_a, down, up, tab = lax.optimization_barrier((mine_a, down, up, tab))
    mine_b = joined([half_b, *ups[1:3], up, far, down, *downs[2:0:-1]])

    down, up = both_ways(mine_a, mine_a, "z", NZ)
    low, high = both_ways(mine_b, mine_b, "x", NX)
    pieces_a = [mine_a, down, up]
    down, up, flat = lax.optimization_barrier((down, up, flat))
    down, up = both_ways(down, up, "z", NZ)
    pieces_a += [down, up]
    norm = norm_of(flat)
    down, up, norm = lax.optimization_barrier((down, up, norm))
    far_b = both_ways(*halves(low, high), "x", NX)
    down, up = both_ways(down, up, "z", NZ)
    pieces_a += [down, up]
    pieces_a += both_ways(*halves(down, up), "z", NZ)
    return pieces_a, [mine_b, low, high, *far_b], flat, norm, tab


def scores_kernel(order, k, tab, refs, weight, norm, *rest):
    arrays = rest[: len(order)]
    outs, (images, parts, whole, scaled, held, near_refs, sems) = (
        rest[len(order) : len(order) + 3],
        rest[len(order) + 3 :],
    )
    copies = fetch(arrays, whole, sems)
    [(refs_copy, _, _)] = fetch([refs], near_refs, sems, len(order))
    for copy, base, count in copies:
        copy.wait()

        def tile(i, carry, base=base):
            rows = pl.ds(pl.multiple_of(base + i * 16, 16), 16)
            scaled[rows, :] = (whole[rows, :].astype(jnp.float32) * weight[...]).astype(
                jnp.bfloat16
            )
            return carry

        lax.fori_loop(0, count // 16, tile, 0)
    images_write = pltpu.make_async_copy(whole, images, sems.at[len(order) + 4])
    images_write.start()
    refs_copy.wait()
    held[...] = (
        lax.dot_general(
            scaled[...],
            near_refs[...],
            (((1,), (1,)), ((), ())),
            preferred_element_type=jnp.float32,
        )
        - norm[...]
    )
    def compact(n, carry):
        slot = tab[k * BLOCKS + n]

        @pl.when(slot >= 0)
        def _():
            for t in range(NY):
                row = n * HALF + tab[4 * BLOCKS + 6 + k * NY + t] * 8
                to = pl.ds(pl.multiple_of(slot * 8, 8) + t * QUARTER, 8)
                parts[to, :] = held[pl.ds(pl.multiple_of(row, 8), 8), :]

        return carry

    lax.fori_loop(0, BLOCKS, compact, 0)
    done = []
    for i, (out, t, count) in enumerate(zip(outs, (2, 0, 1), (2, 1, 1))):
        source = parts.at[pl.ds(t * QUARTER, count * QUARTER), :]
        done.append(pltpu.make_async_copy(source, out, sems.at[len(order) + 1 + i]))
        done[-1].start()
    for copy in done:
        copy.wait()
    images_write.wait()


def partial_scores(order, k, tab, refs, weight, norm, pieces):
    part = jax.ShapeDtypeStruct((QUARTER, REFS), jnp.float32)
    both = jax.ShapeDtypeStruct((2 * QUARTER, REFS), jnp.float32)
    return pl.pallas_call(
        lambda *refs_: scores_kernel(order, k, *refs_),
        out_shape=(both, part, part, jax.ShapeDtypeStruct((1024, COLS), jnp.bfloat16)),
        in_specs=[SMEM, ANY, VMEM, VMEM] + [ANY] * len(pieces),
        out_specs=(ANY, ANY, ANY, ANY),
        scratch_shapes=[
            pltpu.VMEM((NY * QUARTER, REFS), jnp.float32),
            pltpu.VMEM((1024, COLS), jnp.bfloat16),
            pltpu.VMEM((1024, COLS), jnp.bfloat16),
            pltpu.VMEM((1024, REFS), jnp.float32),
            pltpu.VMEM((REFS, COLS), jnp.bfloat16),
            pltpu.SemaphoreType.DMA((len(pieces) + 5,)),
        ],
        compiler_params=pltpu.CompilerParams(vmem_limit_bytes=20 << 20),
        cost_estimate=pl.CostEstimate(
            flops=2 * 1024 * COLS * REFS, bytes_accessed=8 << 20, transcendentals=0
        ),
        name="partial_scores",
    )(tab, refs, weight, norm, *pieces)


def diagonal():
    return lax.broadcasted_iota(jnp.int32, (128, 128), 0) == lax.broadcasted_iota(
        jnp.int32, (128, 128), 1
    )


def local_kernel(kept, a0, a1, a2, b0, b1, b2, probs, stats, high, mass):
    high[...] = jnp.full(high.shape, floor_value, jnp.float32)
    mass[...] = jnp.zeros(mass.shape, jnp.float32)
    parts = []
    for first, second, third in ((a0, a1, a2), (b0, b1, b2)):
        score = first[...] + second[:QUARTER, :] + third[...]
        top = jnp.max(score, axis=1, keepdims=True)
        value = jnp.exp(score - top)
        parts.append((top, value, jnp.sum(value, axis=1, keepdims=True)))
    for j in range(MOST):
        block = kept[j]
        valid = block >= 0
        rows = slice(8 * j, 8 * j + 8)
        both = jnp.concatenate([value[rows] for _, value, _ in parts], axis=0)
        probs[16 * j : 16 * j + 16, :] = jnp.where(valid, both, 0.0).astype(jnp.bfloat16)

        @pl.when(valid)
        def _(block=block, rows=rows):
            for k, (top, _, total) in enumerate(parts):
                at = pl.ds(pl.multiple_of(block * 8, 8) + k * 256, 8)
                high[at, :] = jnp.broadcast_to(top[rows], (8, 128))
                mass[at, :] = jnp.broadcast_to(total[rows], (8, 128))

    eye = diagonal()
    for k, source in enumerate((high, mass)):
        for g in range(4):
            square = source[128 * g : 128 * g + 128, :]
            row = jnp.sum(jnp.where(eye, square, 0.0), axis=0, keepdims=True)
            stats[:, 4 * k + g : 4 * k + g + 1, :] = jnp.broadcast_to(row[None], (BLOCKS, 1, 128))


def local_stats(kept, a, b):
    return pl.pallas_call(
        local_kernel,
        out_shape=(
            jax.ShapeDtypeStruct((MOST * 16, REFS), jnp.bfloat16),
            jax.ShapeDtypeStruct((BLOCKS, 8, 128), jnp.float32),
        ),
        in_specs=[SMEM] + [VMEM] * 6,
        out_specs=(VMEM, VMEM),
        scratch_shapes=[pltpu.VMEM((512, 128), jnp.float32)] * 2,
        compiler_params=pltpu.CompilerParams(vmem_limit_bytes=16 << 20),
        name="local_stats",
    )(kept, *a, *b)


def combine_kernel(everyone, own, out):
    highs, masses = everyone[:, 0:4, :], everyone[:, 4:8, :]
    top = jnp.max(highs, axis=0)
    total = jnp.sum(masses * jnp.exp(highs - top[None]), axis=0)
    log_norm = top + jnp.log(total)
    out[0:4, :] = jnp.exp(own[0, 0:4, :] - log_norm)
    out[4:8, :] = log_norm


def combine(everyone, own):
    return pl.pallas_call(
        combine_kernel,
        out_shape=jax.ShapeDtypeStruct((8, 128), jnp.float32),
        in_specs=[VMEM, VMEM],
        out_specs=VMEM,
        name="combine_stats",
    )(everyone, own)


def fetch_both(first, second, images, sems):
    copies = fetch((first, second), images, sems)
    return [copy for copy, _, _ in copies]


def send_kernel(tab, *rest):
    scales, (own, far, near, top, low, first, second), rest = rest[:4], rest[4:11], rest[11:]
    out, rest_flipped, total, flipped, images, column, dense, probs, sems = rest
    copies = fetch_both(first, second, images, sems)
    cut = MOST * 8
    for i, source in enumerate((own, far, near)):
        probs[i] = source[...]
    probs[3, :cut, :] = top[...]
    probs[3, cut:, :] = low[...]
    eye = diagonal()
    for q, scale in enumerate(scales):
        for g in range(4):
            spread = jnp.broadcast_to(scale[g : g + 1, :], (128, 128))
            one = jnp.sum(jnp.where(eye, spread, 0.0), axis=1, keepdims=True)
            column[q, 128 * g : 128 * g + 128, :] = jnp.broadcast_to(one, (128, 128))
    for k in range(2):

        def fill(n, carry, k=k):
            slot = tab[k * BLOCKS + n]
            block = pl.ds(pl.multiple_of(tab[(2 + k) * BLOCKS + n] * 8, 8) + 256 * k, 8)
            at = pl.multiple_of(jnp.maximum(slot, 0) * 16, 16)
            parts = []
            for q in range(NY):
                owner = tab[4 * BLOCKS + 2 + q]
                value = probs[owner, pl.ds(at, 16), :].astype(jnp.float32)[8 * k : 8 * k + 8]
                factor = column[owner, block, :]
                parts.append(value * jnp.concatenate([factor] * 4, axis=1))
            rows = jnp.where(slot >= 0, jnp.concatenate(parts, axis=0), 0.0)
            dense[pl.ds(pl.multiple_of(n * HALF, HALF), HALF), :] = rows.astype(jnp.bfloat16)
            return carry

        lax.fori_loop(0, BLOCKS, fill, 0)
        flipped[:, 1024 * k : 1024 * k + 1024] = dense[...].T
    own_rows = pl.ds(pl.multiple_of(tab[4 * BLOCKS + 1], 256), 256)
    hand_on = pltpu.make_async_copy(flipped.at[own_rows, :], rest_flipped, sems.at[2])
    hand_on.start()
    for copy in copies:
        copy.wait()
    other_rows = pl.ds(pl.multiple_of(tab[4 * BLOCKS], 256), 256)
    total[...] = jnp.dot(
        flipped[other_rows, :], images[...], preferred_element_type=jnp.float32
    )
    write = pltpu.make_async_copy(total, out, sems.at[3])
    write.start()
    write.wait()
    hand_on.wait()


def keep_kernel(flipped, first, second, out, near_flipped, images, sems):
    own = pltpu.make_async_copy(flipped, near_flipped, sems.at[2])
    own.start()
    copies = fetch_both(first, second, images, sems)
    own.wait()
    for part, copy in enumerate(copies):
        copy.wait()
        span = slice(1024 * part, 1024 * part + 1024)
        value = jnp.dot(
            near_flipped[:, span], images[span, :], preferred_element_type=jnp.float32
        )
        if part == 0:
            out[...] = value
        else:
            out[...] += value


def final_kernel(mine, other, out):
    total = mine[...] + other[...]
    out[:, 0, :] = total[:, : COLS // 2]
    out[:, 1, :] = total[:, COLS // 2 :]


def weighted_sums(tab, scales, probs, images):
    half = jax.ShapeDtypeStruct((REFS // 2, COLS), jnp.float32)
    cost = pl.CostEstimate(
        flops=2 * 2048 * COLS * REFS // 2, bytes_accessed=12 << 20, transcendentals=0
    )
    out, flipped = pl.pallas_call(
        send_kernel,
        out_shape=(half, jax.ShapeDtypeStruct((REFS // 2, COLS), jnp.bfloat16)),
        in_specs=[SMEM] + [VMEM] * 9 + [ANY] * 2,
        out_specs=(ANY, ANY),
        scratch_shapes=[
            pltpu.VMEM((REFS // 2, COLS), jnp.float32),
            pltpu.VMEM((REFS, COLS), jnp.bfloat16),
            pltpu.VMEM((2048, COLS), jnp.bfloat16),
            pltpu.VMEM((NY, 512, 128), jnp.float32),
            pltpu.VMEM((1024, REFS), jnp.bfloat16),
            pltpu.VMEM((NY, MOST * 16, REFS), jnp.bfloat16),
            pltpu.SemaphoreType.DMA((4,)),
        ],
        compiler_params=pltpu.CompilerParams(vmem_limit_bytes=60 << 20),
        cost_estimate=cost,
        name="weighted_send",
    )(tab, *scales, *probs, *images)
    other = lax.ppermute(out, "dom", [(0, 1), (1, 0)])
    mine = pl.pallas_call(
        keep_kernel,
        out_shape=half,
        in_specs=[ANY] * 3,
        out_specs=VMEM,
        scratch_shapes=[
            pltpu.VMEM((REFS // 2, COLS), jnp.bfloat16),
            pltpu.VMEM((2048, COLS), jnp.bfloat16),
            pltpu.SemaphoreType.DMA((3,)),
        ],
        compiler_params=pltpu.CompilerParams(vmem_limit_bytes=60 << 20),
        cost_estimate=cost,
        name="weighted_keep",
    )(flipped, *images)
    return pl.pallas_call(
        final_kernel,
        out_shape=jax.ShapeDtypeStruct((REFS // 2, 2, COLS // 2), jnp.float32),
        in_specs=[VMEM, VMEM],
        out_specs=VMEM,
        compiler_params=pltpu.CompilerParams(vmem_limit_bytes=20 << 20),
        name="both_groups",
    )(mine, other)


def shards(references, images, noise_var, shell_of, kept_blocks):
    z, x = lax.axis_index("z"), lax.axis_index("x")
    d, y = lax.axis_index("dom"), lax.axis_index("shell")
    kept = kept_blocks.reshape(MOST)

    shells = jnp.arange(noise_var.shape[0], dtype=jnp.int32)
    picked = jnp.where(shells[:, None] == shell_of[None, :], noise_var[:, None], 0.0)
    weight = 1.0 / jnp.sum(picked, axis=0)
    weight = jnp.concatenate([weight, weight])

    def norm_of(flat):
        return 0.5 * jnp.sum(weight * jnp.square(flat.astype(jnp.float32)), axis=1)[None, :]

    near, far = y ^ 1, 3 - y
    across = 3 - near
    to_near = [(0, 1), (1, 0), (2, 3), (3, 2)]
    to_far = [(0, 3), (3, 0), (1, 2), (2, 1)]
    to_across = [(0, 2), (2, 0), (1, 3), (3, 1)]

    offsets = [b for order in (ORDER_A, ORDER_B) * 2 for piece in order for b in piece]
    offsets = jnp.array(offsets + [(0, 0)] * 14, jnp.int32)
    block = (z + offsets[:, 0]) % NZ * NX + (x + offsets[:, 1]) % NX
    index = jnp.arange(4 * BLOCKS + 14, dtype=jnp.int32)
    slots = jnp.arange(MOST, dtype=jnp.int32)
    slot = jnp.max(jnp.where(kept[None, :] == block[:, None], slots[None, :], -1), axis=1)
    rank = index - 4 * BLOCKS - 2
    tab = jnp.where(rank == y, 0, jnp.where(rank == far, 1, jnp.where(rank == near, 2, 3)))
    for at, value in enumerate((y, far, near, across, y, near, far, across)):
        tab = jnp.where(rank == NY + at, value, tab)
    tab = jnp.where(rank == -1, d * 256, jnp.where(rank == -2, (1 - d) * 256, tab))
    tab = jnp.where(index < 2 * BLOCKS, slot, jnp.where(index < 4 * BLOCKS, block, tab))

    img = images.reshape(ROWS, COLS)
    pieces_a, pieces_b, refs, norm, tab = gather(
        img[:HALF], img[HALF:], references.reshape(REFS, COLS), norm_of, tab
    )
    weight = weight[None, :]

    def summed(order, k, pieces, first, second):
        send, keep0, keep1, whole = partial_scores(order, k, tab, refs, weight, norm, pieces)
        got = lax.ppermute(send, "shell", first)
        last = lax.ppermute(keep1 + got[QUARTER:], "shell", second)
        return (keep0, got, last), whole

    sum_a, whole_a = summed(ORDER_A, 0, pieces_a, to_near, to_far)
    sum_b, whole_b = summed(ORDER_B, 1, pieces_b, to_far, to_near)

    probs, stats = local_stats(kept, sum_a, sum_b)

    from_near = lax.ppermute(probs, "shell", to_near)
    from_far = lax.ppermute(probs, "shell", to_far)
    top, low = halves(from_far, from_near)
    across_top = lax.ppermute(top, "shell", to_near)
    across_low = lax.ppermute(low, "shell", to_far)
    everyone = lax.all_to_all(
        stats, ("z", "x"), 0, 0, tiled=True
    )
    scale = combine(everyone, stats)
    scales = [scale] + [lax.ppermute(scale, "shell", to) for to in (to_far, to_near, to_across)]
    weighted = weighted_sums(
        tab,
        scales,
        (probs, from_far, from_near, across_top, across_low),
        (whole_a, whole_b),
    )

    log_norms = jnp.stack(scales)[:, 4:8, :].reshape(NY, 2, BLOCKS, 8)
    here = jnp.arange(BLOCKS, dtype=jnp.int32) == z * NX + x
    log_norms = jnp.sum(jnp.where(here[None, None, :, None], log_norms, 0.0), axis=2)
    owners = jnp.stack([y, far, near, across])[None, :] == jnp.arange(NY, dtype=jnp.int32)[:, None]
    log_norm = jnp.sum(jnp.where(owners[:, :, None, None], log_norms[None], 0.0), axis=1)
    log_norm = jnp.transpose(log_norm, (1, 0, 2)).reshape(ROWS)
    return weighted, log_norm


def solution(mesh):
    wide = Mesh(mesh.devices.reshape(NZ, NX, 2, NY), ("z", "x", "dom", "shell"))
    orient = ("z", "x")
    placed = (
        P(orient, None, "shell"),
        P(("z", "x", "dom"), None, "shell"),
        P(),
        P("shell"),
        P(orient, "dom", None),
    )
    return jax.shard_map(
        shards,
        mesh=wide,
        in_specs=placed,
        out_specs=(P(("z", "x", "dom"), None, "shell"), P(("z", "x", "dom"))),
        check_vma=False,
    )
```

profile of v0, /device:TPU:1, one launch (start us, length us, event | category | flops | bytes accessed | tf_op | source)
XLA Modules:
  0.0 167.9 jit_solution(13472168166598159421)
XLA Ops:
  4.5 4.0 %collective-permute-start.6 = (bf16[32,2048]{1,0:T(8,128)(2,1)S(1)}, bf16[32,2048]{1,0:T(8,128)(2,1)S(1)}, u32[]{:S(2)}, u32[]{:S(2)}) collective-permute-start(bf16[32,2048]{1,0:T(8,128)(2,1)S(1)} %bitcast.25), channel_id=1, source_target_pairs={{0,224},{32,0},{64,32},{96,64},{128,96},{160,128},{192,160},{224,1... | collective-permute-start | bytes 393224 | tf_op jit(solution)/shard_map/ppermute | solution.py:34
  8.5 3.1 %collective-permute-done.3.rest_7_ = bf16[32,2048]{1,0:T(8,128)(2,1)S(1)} collective-permute-done((bf16[32,2048]{1,0:T(8,128)(2,1)S(1)}, bf16[32,2048]{1,0:T(8,128)(2,1)S(1)}, u32[]{:S(2)}, u32[]{:S(2)}) %collective-permute-start.3) | collective-permute-done | bytes 131104 | tf_op jit(solution)/shard_map/ppermute | solution.py:34
  16.6 2.7 %collective-permute-start.7 = (bf16[32,2048]{1,0:T(8,128)(2,1)S(1)}, bf16[32,2048]{1,0:T(8,128)(2,1)S(1)}, u32[]{:S(2)}, u32[]{:S(2)}) collective-permute-start(bf16[32,2048]{1,0:T(8,128)(2,1)S(1)} %collective-permute-done.6.rest_1_), channel_id=1, source_target_pairs={{0,224},{32,0},{64,32},{96,64},{128,96},{160,128},{192,160},{224,1... | collective-permute-start | bytes 393224 | tf_op jit(solution)/shard_map/ppermute | solution.py:34
  21.2 3.4 %collective-permute-start.8 = (bf16[32,2048]{1,0:T(8,128)(2,1)S(1)}, bf16[32,2048]{1,0:T(8,128)(2,1)S(1)}, u32[]{:S(2)}, u32[]{:S(2)}) collective-permute-start(bf16[32,2048]{1,0:T(8,128)(2,1)S(1)} %collective-permute-done.7.rest_2_), channel_id=1, source_target_pairs={{0,224},{32,0},{64,32},{96,64},{128,96},{160,128},{192,160},{224,1... | collective-permute-start | bytes 393224 | tf_op jit(solution)/shard_map/ppermute | solution.py:34
  26.6 3.1 %collective-permute-start.10 = (bf16[128,2048]{1,0:T(8,128)(2,1)S(1)}, bf16[128,2048]{1,0:T(8,128)(2,1)S(1)}, u32[]{:S(2)}, u32[]{:S(2)}) collective-permute-start(bf16[128,2048]{1,0:T(8,128)(2,1)S(1)} %joined.2.refs__4_), channel_id=1, source_target_pairs={{0,224},{32,0},{64,32},{96,64},{128,96},{160,128},{192,160},{224,1... | collective-permute-start | bytes 1572872 | tf_op jit(solution)/shard_map/ppermute | solution.py:34
  33.4 3.1 %collective-permute-done.10.refs__6_ = bf16[128,2048]{1,0:T(8,128)(2,1)S(1)} collective-permute-done((bf16[128,2048]{1,0:T(8,128)(2,1)S(1)}, bf16[128,2048]{1,0:T(8,128)(2,1)S(1)}, u32[]{:S(2)}, u32[]{:S(2)}) %collective-permute-start.10) | collective-permute-done | bytes 524320 | tf_op jit(solution)/shard_map/ppermute | solution.py:34
  36.6 3.7 %collective-permute-done.9.refs__5_ = bf16[128,2048]{1,0:T(8,128)(2,1)S(1)} collective-permute-done((bf16[128,2048]{1,0:T(8,128)(2,1)S(1)}, bf16[128,2048]{1,0:T(8,128)(2,1)S(1)}, u32[]{:S(2)}, u32[]{:S(2)}) %collective-permute-start.9) | collective-permute-done | bytes 524320 | tf_op jit(solution)/shard_map/ppermute | solution.py:34
  40.3 2.7 %collective-permute-start.12 = (bf16[128,2048]{1,0:T(8,128)(2,1)S(1)}, bf16[128,2048]{1,0:T(8,128)(2,1)S(1)}, u32[]{:S(2)}, u32[]{:S(2)}) collective-permute-start(bf16[128,2048]{1,0:T(8,128)(2,1)S(1)} %collective-permute-done.10.refs__6_), channel_id=1, source_target_pairs={{0,224},{32,0},{64,32},{96,64},{128,96},{160,128},{192,160},{224,1... | collective-permute-start | bytes 1572872 | tf_op jit(solution)/shard_map/ppermute | solution.py:34
  43.6 7.1 %collective-permute-done.11.refs__7_ = bf16[128,2048]{1,0:T(8,128)(2,1)S(1)} collective-permute-done((bf16[128,2048]{1,0:T(8,128)(2,1)S(1)}, bf16[128,2048]{1,0:T(8,128)(2,1)S(1)}, u32[]{:S(2)}, u32[]{:S(2)}) %collective-permute-start.11) | collective-permute-done | bytes 524320 | tf_op jit(solution)/shard_map/ppermute | solution.py:34
  50.7 2.7 %collective-permute-start.14 = (bf16[128,2048]{1,0:T(8,128)(2,1)S(1)}, bf16[128,2048]{1,0:T(8,128)(2,1)S(1)}, u32[]{:S(2)}, u32[]{:S(2)}) collective-permute-start(bf16[128,2048]{1,0:T(8,128)(2,1)S(1)} %collective-permute-done.12.refs__8_), channel_id=1, source_target_pairs={{0,224},{32,0},{64,32},{96,64},{128,96},{160,128},{192,160},{224,1... | collective-permute-start | bytes 1572872 | tf_op jit(solution)/shard_map/ppermute | solution.py:34
  56.2 5.4 %collective-permute-done.13.first.refs__9_ = bf16[128,2048]{1,0:T(8,128)(2,1)S(1)} collective-permute-done((bf16[128,2048]{1,0:T(8,128)(2,1)S(1)}, bf16[128,2048]{1,0:T(8,128)(2,1)S(1)}, u32[]{:S(2)}, u32[]{:S(2)}) %collective-permute-start.13) | collective-permute-done | bytes 524320 | tf_op jit(solution)/shard_map/ppermute | solution.py:34
  61.8 3.0 %collective-permute-start.16 = (bf16[64,2048]{1,0:T(8,128)(2,1)S(1)}, bf16[64,2048]{1,0:T(8,128)(2,1)S(1)}, u32[]{:S(2)}, u32[]{:S(2)}) collective-permute-start(bf16[64,2048]{1,0:T(8,128)(2,1)S(1)} %get-tuple-element.39), channel_id=1, source_target_pairs={{0,224},{32,0},{64,32},{96,64},{128,96},{160,128},{192,160},{224,1... | collective-permute-start | bytes 786440 | tf_op jit(solution)/shard_map/ppermute | solution.py:34
  64.8 5.7 %partial_scores.3 = (f32[384,512]{1,0:T(8,128)S(1)}, f32[192,512]{1,0:T(8,128)S(1)}, f32[192,512]{1,0:T(8,128)S(1)}, bf16[1024,2048]{1,0:T(8,128)(2,1)S(1)}) custom-call(s32[142]{0:T(256)S(1)} %compare_select_fusion.22.refs__0_.tab, bf16[512,2048]{1,0:T(8,128)(2,1)S(1)} %bitcast.22, f32[1,2048]{1,0:T(1,128)S(1)} %bitcast.31, f32[1,512]{1,0:T(1,128)S(1)} %bitcast.33, ...), custom_call_target="tpu_custom_call" | custom-call | flops 2147483648 | bytes 8388608 | tf_op jit(solution)/shard_map/partial_scores/pallas_call | solution.py:183
  72.6 2.7 %collective-permute-start.24 = (f32[384,512]{1,0:T(8,128)S(1)}, f32[384,512]{1,0:T(8,128)S(1)}, u32[]{:S(2)}, u32[]{:S(2)}) collective-permute-start(f32[384,512]{1,0:T(8,128)S(1)} %get-tuple-element.48), channel_id=1, source_target_pairs={{0,3},{3,0},{1,2},{2,1},{4,7},{7,4},{5,6},{6,5},{8,11},{11,8},{9,1... | collective-permute-start | bytes 2359304 | tf_op jit(solution)/shard_map/ppermute | solution.py:439
  75.4 5.8 %partial_scores.2 = (f32[384,512]{1,0:T(8,128)S(1)}, f32[192,512]{1,0:T(8,128)S(1)}, f32[192,512]{1,0:T(8,128)S(1)}, bf16[1024,2048]{1,0:T(8,128)(2,1)S(1)}) custom-call(s32[142]{0:T(256)S(1)} %compare_select_fusion.22.refs__0_.tab, bf16[512,2048]{1,0:T(8,128)(2,1)S(1)} %bitcast.23, f32[1,2048]{1,0:T(1,128)S(1)} %bitcast.32, f32[1,512]{1,0:T(1,128)S(1)} %bitcast.34, ...), custom_call_target="tpu_custom_call" | custom-call | flops 2147483648 | bytes 8388608 | tf_op jit(solution)/shard_map/partial_scores/pallas_call | solution.py:183
  81.3 3.5 %collective-permute-done.24.b1 = f32[384,512]{1,0:T(8,128)S(1)} collective-permute-done((f32[384,512]{1,0:T(8,128)S(1)}, f32[384,512]{1,0:T(8,128)S(1)}, u32[]{:S(2)}, u32[]{:S(2)}) %collective-permute-start.24) | collective-permute-done | bytes 786464 | tf_op jit(solution)/shard_map/ppermute | solution.py:439
  85.1 7.3 %collective-permute-done.17.a1 = f32[384,512]{1,0:T(8,128)S(1)} collective-permute-done((f32[384,512]{1,0:T(8,128)S(1)}, f32[384,512]{1,0:T(8,128)S(1)}, u32[]{:S(2)}, u32[]{:S(2)}) %collective-permute-start.17) | collective-permute-done | bytes 786464 | tf_op jit(solution)/shard_map/ppermute | solution.py:439
  92.5 5.4 %collective-permute-done.25.b2 = f32[192,512]{1,0:T(8,128)S(1)} collective-permute-done((f32[192,512]{1,0:T(8,128)S(1)}, f32[192,512]{1,0:T(8,128)S(1)}, u32[]{:S(2)}, u32[]{:S(2)}) %collective-permute-start.25) | collective-permute-done | bytes 393248 | tf_op jit(solution)/shard_map/ppermute | solution.py:440
  104.5 7.1 %all-to-all-start = ((f32[32,8,128]{2,1,0:T(8,128)}), f32[32,8,128]{2,1,0:T(8,128)S(1)}, u32[]{:S(2)}, u32[]{:S(2)}) async-start(f32[32,8,128]{2,1,0:T(8,128)} %get-tuple-element.50.own), calls=%async_computation | async-start | bytes 262144 | tf_op jit(solution)/shard_map/all_to_all | solution.py:453
  113.6 2.8 %collective-permute-start.32 = (bf16[192,512]{1,0:T(8,128)(2,1)S(1)}, bf16[192,512]{1,0:T(8,128)(2,1)S(1)}, u32[]{:S(2)}, u32[]{:S(2)}) collective-permute-start(bf16[192,512]{1,0:T(8,128)(2,1)S(1)} %get-tuple-element.53), channel_id=1, source_target_pairs={{0,3},{3,0},{1,2},{2,1},{4,7},{7,4},{5,6},{6,5},{8,11},{11,8},{9,1... | collective-permute-start | bytes 589832 | tf_op jit(solution)/shard_map/ppermute | solution.py:452
  116.4 4.6 %all-to-all-done.everyone = f32[32,8,128]{2,1,0:T(8,128)S(1)} async-done(((f32[32,8,128]{2,1,0:T(8,128)}), f32[32,8,128]{2,1,0:T(8,128)S(1)}, u32[]{:S(2)}, u32[]{:S(2)}) %all-to-all-start) | async-done | bytes 131104 | tf_op jit(solution)/shard_map/all_to_all | solution.py:453
  129.0 8.8 %weighted_send.1 = (f32[256,2048]{1,0:T(8,128)}, bf16[256,2048]{1,0:T(8,128)(2,1)}) custom-call(s32[142]{0:T(256)} %copy-done.6, f32[8,128]{1,0:T(8,128)} %combine_stats.1.rest_0_, f32[8,128]{1,0:T(8,128)} %copy-done.15, f32[8,128]{1,0:T(8,128)} %copy-done.14, f32[8,128]{1,0:T(8,128)} %copy-done.13, bf16[384,512]{1,0:T(8,128)(2,1)} %copy-done.5, ...), custom_call_target="tpu_custom_call" | custom-call | flops 2147483648 | bytes 12582912 | tf_op jit(solution)/shard_map/weighted_send/pallas_call | solution.py:356
  137.8 18.6 %collective-permute-start.33 = (f32[256,2048]{1,0:T(8,128)}, f32[256,2048]{1,0:T(8,128)S(1)}, u32[]{:S(2)}, u32[]{:S(2)}) collective-permute-start(f32[256,2048]{1,0:T(8,128)} %get-tuple-element.57), channel_id=1, source_target_pairs={{0,4},{4,0},{1,5},{5,1},{2,6},{6,2},{3,7},{7,3},{8,12},{12,8},{9,1... | collective-permute-start | bytes 6291464 | tf_op jit(solution)/shard_map/ppermute | solution.py:374
  158.1 6.4 %weighted_keep.1.mine = f32[256,2048]{1,0:T(8,128)} custom-call(bf16[256,2048]{1,0:T(8,128)(2,1)} %get-tuple-element.56.flipped, bf16[1024,2048]{1,0:T(8,128)(2,1)} %copy-done.1, bf16[1024,2048]{1,0:T(8,128)(2,1)} %copy-done), custom_call_target="tpu_custom_call" | custom-call | flops 2147483648 | bytes 12582912 | tf_op jit(solution)/shard_map/weighted_keep/pallas_call | solution.py:375
  (118 shorter events, 44.2 us)
Async XLA Ops:
  4.5 12.1 %collective-permute-start.6 = (bf16[32,2048]{1,0:T(8,128)(2,1)S(1)}, bf16[32,2048]{1,0:T(8,128)(2,1)S(1)}, u32[]{:S(2)}, u32[]{:S(2)}) collective-permute-start(bf16[32,2048]{1,0:T(8,128)(2,1)S(1)} %bitcast.25), channel_id=1, source_target_pairs={{0,224},{32,0},{64,32},{96,64},{128,96},{160,128},{192,160},{224,1... | collective-permute-start | bytes 393224 | tf_op jit(solution)/shard_map/ppermute | solution.py:34
  11.7 12.9 %collective-permute-start.2 = (bf16[32,2048]{1,0:T(8,128)(2,1)S(1)}, bf16[32,2048]{1,0:T(8,128)(2,1)S(1)}, u32[]{:S(2)}, u32[]{:S(2)}) collective-permute-start(bf16[32,2048]{1,0:T(8,128)(2,1)S(1)} %bitcast.27), channel_id=1, source_target_pairs={{0,8},{8,16},{16,24},{24,0},{1,9},{9,17},{17,25},{25,1},{2,10},{10... | collective-permute-start | bytes 393224 | tf_op jit(solution)/shard_map/ppermute | solution.py:34
  13.0 11.7 %collective-permute-start.1 = (bf16[32,2048]{1,0:T(8,128)(2,1)S(1)}, bf16[32,2048]{1,0:T(8,128)(2,1)S(1)}, u32[]{:S(2)}, u32[]{:S(2)}) collective-permute-start(bf16[32,2048]{1,0:T(8,128)(2,1)S(1)} %bitcast.28), channel_id=1, source_target_pairs={{0,16},{8,24},{16,0},{24,8},{1,17},{9,25},{17,1},{25,9},{2,18},{10... | collective-permute-start | bytes 393224 | tf_op jit(solution)/shard_map/ppermute | solution.py:34
  26.6 10.0 %collective-permute-start.10 = (bf16[128,2048]{1,0:T(8,128)(2,1)S(1)}, bf16[128,2048]{1,0:T(8,128)(2,1)S(1)}, u32[]{:S(2)}, u32[]{:S(2)}) collective-permute-start(bf16[128,2048]{1,0:T(8,128)(2,1)S(1)} %joined.2.refs__4_), channel_id=1, source_target_pairs={{0,224},{32,0},{64,32},{96,64},{128,96},{160,128},{192,160},{224,1... | collective-permute-start | bytes 1572872 | tf_op jit(solution)/shard_map/ppermute | solution.py:34
  29.6 10.6 %collective-permute-start.9 = (bf16[128,2048]{1,0:T(8,128)(2,1)S(1)}, bf16[128,2048]{1,0:T(8,128)(2,1)S(1)}, u32[]{:S(2)}, u32[]{:S(2)}) collective-permute-start(bf16[128,2048]{1,0:T(8,128)(2,1)S(1)} %joined.2.refs__4_), channel_id=1, source_target_pairs={{0,32},{32,64},{64,96},{96,128},{128,160},{160,192},{192,224},{224... | collective-permute-start | bytes 1572872 | tf_op jit(solution)/shard_map/ppermute | solution.py:34
  31.1 22.3 %collective-permute-start.21 = (bf16[256,2048]{1,0:T(8,128)(2,1)S(1)}, bf16[256,2048]{1,0:T(8,128)(2,1)S(1)}, u32[]{:S(2)}, u32[]{:S(2)}) collective-permute-start(bf16[256,2048]{1,0:T(8,128)(2,1)S(1)} %joined.3.refs__4_), channel_id=1, source_target_pairs={{0,24},{8,0},{16,8},{24,16},{1,25},{9,1},{17,9},{25,17},{2,26},{10... | collective-permute-start | bytes 3145736 | tf_op jit(solution)/shard_map/ppermute | solution.py:34
  31.2 22.3 %collective-permute-start.20 = (bf16[256,2048]{1,0:T(8,128)(2,1)S(1)}, bf16[256,2048]{1,0:T(8,128)(2,1)S(1)}, u32[]{:S(2)}, u32[]{:S(2)}) collective-permute-start(bf16[256,2048]{1,0:T(8,128)(2,1)S(1)} %joined.3.refs__4_), channel_id=1, source_target_pairs={{0,8},{8,16},{16,24},{24,0},{1,9},{9,17},{17,25},{25,1},{2,10},{10... | collective-permute-start | bytes 3145736 | tf_op jit(solution)/shard_map/ppermute | solution.py:34
  40.3 10.5 %collective-permute-start.11 = (bf16[128,2048]{1,0:T(8,128)(2,1)S(1)}, bf16[128,2048]{1,0:T(8,128)(2,1)S(1)}, u32[]{:S(2)}, u32[]{:S(2)}) collective-permute-start(bf16[128,2048]{1,0:T(8,128)(2,1)S(1)} %collective-permute-done.9.refs__5_), channel_id=1, source_target_pairs={{0,32},{32,64},{64,96},{96,128},{128,160},{160,192},{192,224},{224... | collective-permute-start | bytes 1572872 | tf_op jit(solution)/shard_map/ppermute | solution.py:34
  40.3 10.5 %collective-permute-start.12 = (bf16[128,2048]{1,0:T(8,128)(2,1)S(1)}, bf16[128,2048]{1,0:T(8,128)(2,1)S(1)}, u32[]{:S(2)}, u32[]{:S(2)}) collective-permute-start(bf16[128,2048]{1,0:T(8,128)(2,1)S(1)} %collective-permute-done.10.refs__6_), channel_id=1, source_target_pairs={{0,224},{32,0},{64,32},{96,64},{128,96},{160,128},{192,160},{224,1... | collective-permute-start | bytes 1572872 | tf_op jit(solution)/shard_map/ppermute | solution.py:34
  50.7 10.9 %collective-permute-start.13 = (bf16[128,2048]{1,0:T(8,128)(2,1)S(1)}, bf16[128,2048]{1,0:T(8,128)(2,1)S(1)}, u32[]{:S(2)}, u32[]{:S(2)}) collective-permute-start(bf16[128,2048]{1,0:T(8,128)(2,1)S(1)} %collective-permute-done.11.refs__7_), channel_id=1, source_target_pairs={{0,32},{32,64},{64,96},{96,128},{128,160},{160,192},{192,224},{224... | collective-permute-start | bytes 1572872 | tf_op jit(solution)/shard_map/ppermute | solution.py:34
  50.7 10.9 %collective-permute-start.14 = (bf16[128,2048]{1,0:T(8,128)(2,1)S(1)}, bf16[128,2048]{1,0:T(8,128)(2,1)S(1)}, u32[]{:S(2)}, u32[]{:S(2)}) collective-permute-start(bf16[128,2048]{1,0:T(8,128)(2,1)S(1)} %collective-permute-done.12.refs__8_), channel_id=1, source_target_pairs={{0,224},{32,0},{64,32},{96,64},{128,96},{160,128},{192,160},{224,1... | collective-permute-start | bytes 1572872 | tf_op jit(solution)/shard_map/ppermute | solution.py:34
  53.5 11.4 %collective-permute-start.22 = (bf16[128,2048]{1,0:T(8,128)(2,1)S(1)}, bf16[128,2048]{1,0:T(8,128)(2,1)S(1)}, u32[]{:S(2)}, u32[]{:S(2)}) collective-permute-start(bf16[128,2048]{1,0:T(8,128)(2,1)S(1)} %get-tuple-element.45), channel_id=1, source_target_pairs={{0,8},{8,16},{16,24},{24,0},{1,9},{9,17},{17,25},{25,1},{2,10},{10... | collective-permute-start | bytes 1572872 | tf_op jit(solution)/shard_map/ppermute | solution.py:34
  53.6 11.3 %collective-permute-start.23 = (bf16[128,2048]{1,0:T(8,128)(2,1)S(1)}, bf16[128,2048]{1,0:T(8,128)(2,1)S(1)}, u32[]{:S(2)}, u32[]{:S(2)}) collective-permute-start(bf16[128,2048]{1,0:T(8,128)(2,1)S(1)} %get-tuple-element.46), channel_id=1, source_target_pairs={{0,24},{8,0},{16,8},{24,16},{1,25},{9,1},{17,9},{25,17},{2,26},{10... | collective-permute-start | bytes 1572872 | tf_op jit(solution)/shard_map/ppermute | solution.py:34
  61.7 13.6 %collective-permute-start.15 = (bf16[64,2048]{1,0:T(8,128)(2,1)S(1)}, bf16[64,2048]{1,0:T(8,128)(2,1)S(1)}, u32[]{:S(2)}, u32[]{:S(2)}) collective-permute-start(bf16[64,2048]{1,0:T(8,128)(2,1)S(1)} %get-tuple-element.38), channel_id=1, source_target_pairs={{0,32},{32,64},{64,96},{96,128},{128,160},{160,192},{192,224},{224... | collective-permute-start | bytes 786440 | tf_op jit(solution)/shard_map/ppermute | solution.py:34
  61.8 13.5 %collective-permute-start.16 = (bf16[64,2048]{1,0:T(8,128)(2,1)S(1)}, bf16[64,2048]{1,0:T(8,128)(2,1)S(1)}, u32[]{:S(2)}, u32[]{:S(2)}) collective-permute-start(bf16[64,2048]{1,0:T(8,128)(2,1)S(1)} %get-tuple-element.39), channel_id=1, source_target_pairs={{0,224},{32,0},{64,32},{96,64},{128,96},{160,128},{192,160},{224,1... | collective-permute-start | bytes 786440 | tf_op jit(solution)/shard_map/ppermute | solution.py:34
  72.6 12.1 %collective-permute-start.24 = (f32[384,512]{1,0:T(8,128)S(1)}, f32[384,512]{1,0:T(8,128)S(1)}, u32[]{:S(2)}, u32[]{:S(2)}) collective-permute-start(f32[384,512]{1,0:T(8,128)S(1)} %get-tuple-element.48), channel_id=1, source_target_pairs={{0,3},{3,0},{1,2},{2,1},{4,7},{7,4},{5,6},{6,5},{8,11},{11,8},{9,1... | collective-permute-start | bytes 2359304 | tf_op jit(solution)/shard_map/ppermute | solution.py:439
  81.2 11.2 %collective-permute-start.17 = (f32[384,512]{1,0:T(8,128)S(1)}, f32[384,512]{1,0:T(8,128)S(1)}, u32[]{:S(2)}, u32[]{:S(2)}) collective-permute-start(f32[384,512]{1,0:T(8,128)S(1)} %get-tuple-element.41), channel_id=1, source_target_pairs={{0,1},{1,0},{2,3},{3,2},{4,5},{5,4},{6,7},{7,6},{8,9},{9,8},{10,11... | collective-permute-start | bytes 2359304 | tf_op jit(solution)/shard_map/ppermute | solution.py:439
  84.8 13.2 %collective-permute-start.25 = (f32[192,512]{1,0:T(8,128)S(1)}, f32[192,512]{1,0:T(8,128)S(1)}, u32[]{:S(2)}, u32[]{:S(2)}) collective-permute-start(f32[192,512]{1,0:T(8,128)S(1)} %slice_add_fusion), channel_id=1, source_target_pairs={{0,1},{1,0},{2,3},{3,2},{4,5},{5,4},{6,7},{7,6},{8,9},{9,8},{10,11... | collective-permute-start | bytes 1179656 | tf_op jit(solution)/shard_map/ppermute | solution.py:440
  102.2 11.2 %collective-permute-start.30 = (bf16[384,512]{1,0:T(8,128)(2,1)S(1)}, bf16[384,512]{1,0:T(8,128)(2,1)S(1)}, u32[]{:S(2)}, u32[]{:S(2)}) collective-permute-start(bf16[384,512]{1,0:T(8,128)(2,1)S(1)} %get-tuple-element.51.rest_4_), channel_id=1, source_target_pairs={{0,1},{1,0},{2,3},{3,2},{4,5},{5,4},{6,7},{7,6},{8,9},{9,8},{10,11... | collective-permute-start | bytes 1179656 | tf_op jit(solution)/shard_map/ppermute | solution.py:448
  102.2 11.2 %collective-permute-start.29 = (bf16[384,512]{1,0:T(8,128)(2,1)S(1)}, bf16[384,512]{1,0:T(8,128)(2,1)S(1)}, u32[]{:S(2)}, u32[]{:S(2)}) collective-permute-start(bf16[384,512]{1,0:T(8,128)(2,1)S(1)} %get-tuple-element.51.rest_4_), channel_id=1, source_target_pairs={{0,3},{3,0},{1,2},{2,1},{4,7},{7,4},{5,6},{6,5},{8,11},{11,8},{9,1... | collective-permute-start | bytes 1179656 | tf_op jit(solution)/shard_map/ppermute | solution.py:449
  104.5 16.5 %all-to-all-start = ((f32[32,8,128]{2,1,0:T(8,128)}), f32[32,8,128]{2,1,0:T(8,128)S(1)}, u32[]{:S(2)}, u32[]{:S(2)}) async-start(f32[32,8,128]{2,1,0:T(8,128)} %get-tuple-element.50.own), calls=%async_computation | async-start | bytes 262144 | tf_op jit(solution)/shard_map/all_to_all | solution.py:453
  113.4 14.8 %collective-permute-start.31 = (bf16[192,512]{1,0:T(8,128)(2,1)S(1)}, bf16[192,512]{1,0:T(8,128)(2,1)S(1)}, u32[]{:S(2)}, u32[]{:S(2)}) collective-permute-start(bf16[192,512]{1,0:T(8,128)(2,1)S(1)} %get-tuple-element.52), channel_id=1, source_target_pairs={{0,1},{1,0},{2,3},{3,2},{4,5},{5,4},{6,7},{7,6},{8,9},{9,8},{10,11... | collective-permute-start | bytes 589832 | tf_op jit(solution)/shard_map/ppermute | solution.py:451
  113.6 14.7 %collective-permute-start.32 = (bf16[192,512]{1,0:T(8,128)(2,1)S(1)}, bf16[192,512]{1,0:T(8,128)(2,1)S(1)}, u32[]{:S(2)}, u32[]{:S(2)}) collective-permute-start(bf16[192,512]{1,0:T(8,128)(2,1)S(1)} %get-tuple-element.53), channel_id=1, source_target_pairs={{0,3},{3,0},{1,2},{2,1},{4,7},{7,4},{5,6},{6,5},{8,11},{11,8},{9,1... | collective-permute-start | bytes 589832 | tf_op jit(solution)/shard_map/ppermute | solution.py:452
  137.8 26.7 %collective-permute-start.33 = (f32[256,2048]{1,0:T(8,128)}, f32[256,2048]{1,0:T(8,128)S(1)}, u32[]{:S(2)}, u32[]{:S(2)}) collective-permute-start(f32[256,2048]{1,0:T(8,128)} %get-tuple-element.57), channel_id=1, source_target_pairs={{0,4},{4,0},{1,5},{5,1},{2,6},{6,2},{3,7},{7,3},{8,12},{12,8},{9,1... | collective-permute-start | bytes 6291464 | tf_op jit(solution)/shard_map/ppermute | solution.py:374
  (29 other events, 281.7 us)
where the time goes:
time: 168 us
  starting transfers between devices  70.9 us (42%)
  waiting for transfers between devices  50.8 us (30%)
  Pallas kernels  34.1 us (20%)
  local copies, waits for them, and re-layouts  7.76 us (5%)
  other arithmetic  3.31 us (2%)
    ppermute x22, starting transfers between devices, step(): lax.ppermute(value, axis, [(i, (i + by) % count) for i in range(count)])  33.4 us
    ppermute x22, waiting for transfers between devices, step(): lax.ppermute(value, axis, [(i, (i + by) % count) for i in range(count)])  24.2 us
    ppermute x1, starting transfers between devices, weighted_sums(): other = lax.ppermute(out, 'dom', [(0, 1), (1, 0)])  18.6 us
    pallas_call x2, Pallas kernels, partial_scores(): pl.pallas_call(lambda *refs_: scores_kernel(order, k, *refs_), out_shape=...  11.5 us
    ppermute x2, waiting for transfers between devices, summed(): got = lax.ppermute(send, 'shell', first)  10.7 us
    pallas_call x1, Pallas kernels, weighted_sums(): pl.pallas_call(send_kernel, out_shape=(half, jax.ShapeDtypeStruct((REFS /...  8.76 us
    ppermute x2, waiting for transfers between devices, summed(): last = lax.ppermute(keep1 + got[QUARTER:], 'shell', second)  7.82 us
    all_to_all x1, starting transfers between devices, shards(): everyone = lax.all_to_all(stats, ('z', 'x'), 0, 0, tiled=True)  7.12 us
  transfers between devices with their start and end apart: 35, of which 15 were waited for; matrix products, arithmetic and copies ran while one was open for 3% of the time, Pallas kernels for 13%

commit v1 on v0

--- a/solution.py
+++ b/solution.py
@@ -193,7 +193,7 @@
             pltpu.VMEM((REFS, COLS), jnp.bfloat16),
             pltpu.SemaphoreType.DMA((len(pieces) + 5,)),
         ],
-        compiler_params=pltpu.CompilerParams(vmem_limit_bytes=20 << 20),
+        compiler_params=pltpu.CompilerParams(vmem_limit_bytes=44 << 20),
         cost_estimate=pl.CostEstimate(
             flops=2 * 1024 * COLS * REFS, bytes_accessed=8 << 20, transcendentals=0
         ),
@@ -268,24 +268,49 @@
         out_shape=jax.ShapeDtypeStruct((8, 128), jnp.float32),
         in_specs=[VMEM, VMEM],
         out_specs=VMEM,
+        compiler_params=pltpu.CompilerParams(vmem_limit_bytes=4 << 20),
         name="combine_stats",
     )(everyone, own)
 
 
-def fetch_both(first, second, images, sems):
-    copies = fetch((first, second), images, sems)
-    return [copy for copy, _, _ in copies]
-
-
-def send_kernel(tab, *rest):
-    scales, (own, far, near, top, low, first, second), rest = rest[:4], rest[4:11], rest[11:]
-    out, rest_flipped, total, flipped, images, column, dense, probs, sems = rest
-    copies = fetch_both(first, second, images, sems)
+def lay_kernel(tab, own, far, near, top, low, first, second, flipped, images, dense, probs, sems):
+    copies = [copy for copy, _, _ in fetch((first, second), images, sems)]
     cut = MOST * 8
     for i, source in enumerate((own, far, near)):
         probs[i] = source[...]
     probs[3, :cut, :] = top[...]
     probs[3, cut:, :] = low[...]
+    for k in range(2):
+
+        def fill(n, carry, k=k):
+            slot = tab[k * BLOCKS + n]
+            at = pl.ds(pl.multiple_of(jnp.maximum(slot, 0) * 16, 16), 16)
+            parts = []
+            for q in range(NY):
+                owner = tab[4 * BLOCKS + 2 + q]
+                parts.append(probs[owner, at, :].astype(jnp.float32)[8 * k : 8 * k + 8])
+            rows = jnp.where(slot >= 0, jnp.concatenate(parts, axis=0), 0.0)
+            dense[pl.ds(pl.multiple_of(n * HALF, HALF), HALF), :] = rows.astype(jnp.bfloat16)
+            return carry
+
+        lax.fori_loop(0, BLOCKS, fill, 0)
+        flipped[:, 1024 * k : 1024 * k + 1024] = dense[...].T
+    for copy in copies:
+        copy.wait()
+
+
+def scaled_rows(flipped, factor, base, out):
+    def tile(i, carry):
+        at = pl.multiple_of(i * 16, 16)
+        rows = flipped[pl.ds(pl.multiple_of(base + at, 16), 16), :].astype(jnp.float32)
+        out[pl.ds(at, 16), :] = (rows * factor[...]).astype(jnp.bfloat16)
+        return carry
+
+    lax.fori_loop(0, REFS // 32, tile, 0)
+
+
+def send_kernel(tab, *rest):
+    scales, (flipped, images, out, factor, total, half, column, ordered, sem) = rest[:4], rest[4:]
     eye = diagonal()
     for q, scale in enumerate(scales):
         for g in range(4):
@@ -295,105 +320,120 @@
     for k in range(2):
 
         def fill(n, carry, k=k):
-            slot = tab[k * BLOCKS + n]
-            block = pl.ds(pl.multiple_of(tab[(2 + k) * BLOCKS + n] * 8, 8) + 256 * k, 8)
-            at = pl.multiple_of(jnp.maximum(slot, 0) * 16, 16)
-            parts = []
+            block = pl.multiple_of(tab[(2 + k) * BLOCKS + n] * 8, 8) + 256 * k
             for q in range(NY):
-                owner = tab[4 * BLOCKS + 2 + q]
-                value = probs[owner, pl.ds(at, 16), :].astype(jnp.float32)[8 * k : 8 * k + 8]
-                factor = column[owner, block, :]
-                parts.append(value * jnp.concatenate([factor] * 4, axis=1))
-            rows = jnp.where(slot >= 0, jnp.concatenate(parts, axis=0), 0.0)
-            dense[pl.ds(pl.multiple_of(n * HALF, HALF), HALF), :] = rows.astype(jnp.bfloat16)
+                to = pl.multiple_of(n * HALF, HALF) + 1024 * k + 8 * q
+                ordered[pl.ds(to, 8), :] = column[
+                    tab[4 * BLOCKS + 2 + q], pl.ds(block, 8), :
+                ]
             return carry
 
         lax.fori_loop(0, BLOCKS, fill, 0)
-        flipped[:, 1024 * k : 1024 * k + 1024] = dense[...].T
-    own_rows = pl.ds(pl.multiple_of(tab[4 * BLOCKS + 1], 256), 256)
-    hand_on = pltpu.make_async_copy(flipped.at[own_rows, :], rest_flipped, sems.at[2])
-    hand_on.start()
-    for copy in copies:
-        copy.wait()
-    other_rows = pl.ds(pl.multiple_of(tab[4 * BLOCKS], 256), 256)
-    total[...] = jnp.dot(
-        flipped[other_rows, :], images[...], preferred_element_type=jnp.float32
-    )
-    write = pltpu.make_async_copy(total, out, sems.at[3])
+    for g in range(16):
+        square = ordered[128 * g : 128 * g + 128, :]
+        factor[:, 128 * g : 128 * g + 128] = jnp.sum(
+            jnp.where(eye, square, 0.0), axis=0, keepdims=True
+        )
+    scaled_rows(flipped, factor, tab[4 * BLOCKS], half)
+    total[...] = jnp.dot(half[...], images[...], preferred_element_type=jnp.float32)
+    write = pltpu.make_async_copy(total, out, sem)
     write.start()
     write.wait()
-    hand_on.wait()
-
-
-def keep_kernel(flipped, first, second, out, near_flipped, images, sems):
-    own = pltpu.make_async_copy(flipped, near_flipped, sems.at[2])
-    own.start()
-    copies = fetch_both(first, second, images, sems)
-    own.wait()
-    for part, copy in enumerate(copies):
+
+
+def keep_kernel(tab, *rest):
+    scales, (flipped, images, factor, out, norms, half) = rest[:4], rest[4:]
+    scaled_rows(flipped, factor, tab[4 * BLOCKS + 1], half)
+    out[...] = jnp.dot(half[...], images[...], preferred_element_type=jnp.float32)
+    home = tab[4 * BLOCKS + 14]
+    lane = lax.broadcasted_iota(jnp.int32, (1, 128), 1)
+    spot = home % 16
+    total = jnp.zeros((1, 128), jnp.float32)
+    for k in range(2):
+        for i, scale in enumerate(scales):
+            first, second = scale[4 + 2 * k : 5 + 2 * k, :], scale[5 + 2 * k : 6 + 2 * k, :]
+            row = jnp.where(home >= 16, second, first)
+            row = jnp.where(lane // 8 == spot, row, 0.0)
+            q = tab[4 * BLOCKS + 6 + i]
+            total += pltpu.roll(row, (HALF * k + q * 8 + 128 - spot * 8) % 128, 1)
+    norms[...] = total[:, :ROWS]
+
+
+def final_kernel(mine, other, out, near, sems):
+    copies = []
+    for i in range(4):
+        rows = pl.ds(64 * i, 64)
+        copies.append(pltpu.make_async_copy(other.at[rows, :], near.at[rows, :], sems.at[i]))
+        copies[-1].start()
+    for i, copy in enumerate(copies):
         copy.wait()
-        span = slice(1024 * part, 1024 * part + 1024)
-        value = jnp.dot(
-            near_flipped[:, span], images[span, :], preferred_element_type=jnp.float32
-        )
-        if part == 0:
-            out[...] = value
-        else:
-            out[...] += value
-
-
-def final_kernel(mine, other, out):
-    total = mine[...] + other[...]
-    out[:, 0, :] = total[:, : COLS // 2]
-    out[:, 1, :] = total[:, COLS // 2 :]
-
-
-def weighted_sums(tab, scales, probs, images):
+        rows = slice(64 * i, 64 * i + 64)
+        total = mine[rows, :] + near[rows, :]
+        out[rows, 0, :] = total[:, : COLS // 2]
+        out[rows, 1, :] = total[:, COLS // 2 :]
+
+
+def weighted_sums(tab, scales, probs, pieces):
     half = jax.ShapeDtypeStruct((REFS // 2, COLS), jnp.float32)
     cost = pl.CostEstimate(
         flops=2 * 2048 * COLS * REFS // 2, bytes_accessed=12 << 20, transcendentals=0
     )
-    out, flipped = pl.pallas_call(
+    flipped, images = pl.pallas_call(
+        lay_kernel,
+        out_shape=(
+            jax.ShapeDtypeStruct((REFS, COLS), jnp.bfloat16),
+            jax.ShapeDtypeStruct((2048, COLS), jnp.bfloat16),
+        ),
+        in_specs=[SMEM] + [VMEM] * 5 + [ANY] * 2,
+        out_specs=(VMEM, VMEM),
+        scratch_shapes=[
+            pltpu.VMEM((1024, REFS), jnp.bfloat16),
+            pltpu.VMEM((NY, MOST * 16, REFS), jnp.bfloat16),
+            pltpu.SemaphoreType.DMA((2,)),
+        ],
+        compiler_params=pltpu.CompilerParams(vmem_limit_bytes=16 << 20),
+        name="lay_posteriors",
+    )(tab, *probs, *pieces)
+    out, factor = pl.pallas_call(
         send_kernel,
-        out_shape=(half, jax.ShapeDtypeStruct((REFS // 2, COLS), jnp.bfloat16)),
-        in_specs=[SMEM] + [VMEM] * 9 + [ANY] * 2,
-        out_specs=(ANY, ANY),
+        out_shape=(half, jax.ShapeDtypeStruct((1, COLS), jnp.float32)),
+        in_specs=[SMEM] + [VMEM] * 6,
+        out_specs=(ANY, VMEM),
         scratch_shapes=[
             pltpu.VMEM((REFS // 2, COLS), jnp.float32),
-            pltpu.VMEM((REFS, COLS), jnp.bfloat16),
-            pltpu.VMEM((2048, COLS), jnp.bfloat16),
+            pltpu.VMEM((REFS // 2, COLS), jnp.bfloat16),
             pltpu.VMEM((NY, 512, 128), jnp.float32),
-            pltpu.VMEM((1024, REFS), jnp.bfloat16),
-            pltpu.VMEM((NY, MOST * 16, REFS), jnp.bfloat16),
+            pltpu.VMEM((2048, 128), jnp.float32),
+            pltpu.SemaphoreType.DMA,
+        ],
+        compiler_params=pltpu.CompilerParams(vmem_limit_bytes=16 << 20),
+        cost_estimate=cost,
+        name="weighted_send",
+    )(tab, *scales, flipped, images)
+    other = lax.ppermute(out, "dom", [(0, 1), (1, 0)])
+    mine, norms = pl.pallas_call(
+        keep_kernel,
+        out_shape=(half, jax.ShapeDtypeStruct((1, ROWS), jnp.float32)),
+        in_specs=[SMEM] + [VMEM] * 7,
+        out_specs=(VMEM, VMEM),
+        scratch_shapes=[pltpu.VMEM((REFS // 2, COLS), jnp.bfloat16)],
+        compiler_params=pltpu.CompilerParams(vmem_limit_bytes=16 << 20),
+        cost_estimate=cost,
+        name="weighted_keep",
+    )(tab, *scales, flipped, images, factor)
+    weighted = pl.pallas_call(
+        final_kernel,
+        out_shape=jax.ShapeDtypeStruct((REFS // 2, 2, COLS // 2), jnp.float32),
+        in_specs=[VMEM, ANY],
+        out_specs=VMEM,
+        scratch_shapes=[
+            pltpu.VMEM((REFS // 2, COLS), jnp.float32),
             pltpu.SemaphoreType.DMA((4,)),
         ],
-        compiler_params=pltpu.CompilerParams(vmem_limit_bytes=60 << 20),
-        cost_estimate=cost,
-        name="weighted_send",
-    )(tab, *scales, *probs, *images)
-    other = lax.ppermute(out, "dom", [(0, 1), (1, 0)])
-    mine = pl.pallas_call(
-        keep_kernel,
-        out_shape=half,
-        in_specs=[ANY] * 3,
-        out_specs=VMEM,
-        scratch_shapes=[
-            pltpu.VMEM((REFS // 2, COLS), jnp.bfloat16),
-            pltpu.VMEM((2048, COLS), jnp.bfloat16),
-            pltpu.SemaphoreType.DMA((3,)),
-        ],
-        compiler_params=pltpu.CompilerParams(vmem_limit_bytes=60 << 20),
-        cost_estimate=cost,
-        name="weighted_keep",
-    )(flipped, *images)
-    return pl.pallas_call(
-        final_kernel,
-        out_shape=jax.ShapeDtypeStruct((REFS // 2, 2, COLS // 2), jnp.float32),
-        in_specs=[VMEM, VMEM],
-        out_specs=VMEM,
-        compiler_params=pltpu.CompilerParams(vmem_limit_bytes=20 << 20),
+        compiler_params=pltpu.CompilerParams(vmem_limit_bytes=16 << 20),
         name="both_groups",
     )(mine, other)
+    return weighted, norms.reshape(ROWS)
 
 
 def shards(references, images, noise_var, shell_of, kept_blocks):
@@ -416,14 +456,16 @@
     to_across = [(0, 2), (2, 0), (1, 3), (3, 1)]
 
     offsets = [b for order in (ORDER_A, ORDER_B) * 2 for piece in order for b in piece]
-    offsets = jnp.array(offsets + [(0, 0)] * 14, jnp.int32)
+    offsets = jnp.array(offsets + [(0, 0)] * 15, jnp.int32)
     block = (z + offsets[:, 0]) % NZ * NX + (x + offsets[:, 1]) % NX
-    index = jnp.arange(4 * BLOCKS + 14, dtype=jnp.int32)
+    index = jnp.arange(4 * BLOCKS + 15, dtype=jnp.int32)
     slots = jnp.arange(MOST, dtype=jnp.int32)
     slot = jnp.max(jnp.where(kept[None, :] == block[:, None], slots[None, :], -1), axis=1)
     rank = index - 4 * BLOCKS - 2
     tab = jnp.where(rank == y, 0, jnp.where(rank == far, 1, jnp.where(rank == near, 2, 3)))
-    for at, value in enumerate((y, far, near, across, y, near, far, across)):
+    for at, value in enumerate(
+        (y, far, near, across, y, near, far, across, z * NX + x)
+    ):
         tab = jnp.where(rank == NY + at, value, tab)
     tab = jnp.where(rank == -1, d * 256, jnp.where(rank == -2, (1 - d) * 256, tab))
     tab = jnp.where(index < 2 * BLOCKS, slot, jnp.where(index < 4 * BLOCKS, block, tab))
@@ -455,20 +497,12 @@
     )
     scale = combine(everyone, stats)
     scales = [scale] + [lax.ppermute(scale, "shell", to) for to in (to_far, to_near, to_across)]
-    weighted = weighted_sums(
+    return weighted_sums(
         tab,
         scales,
         (probs, from_far, from_near, across_top, across_low),
         (whole_a, whole_b),
     )
-
-    log_norms = jnp.stack(scales)[:, 4:8, :].reshape(NY, 2, BLOCKS, 8)
-    here = jnp.arange(BLOCKS, dtype=jnp.int32) == z * NX + x
-    log_norms = jnp.sum(jnp.where(here[None, None, :, None], log_norms, 0.0), axis=2)
-    owners = jnp.stack([y, far, near, across])[None, :] == jnp.arange(NY, dtype=jnp.int32)[:, None]
-    log_norm = jnp.sum(jnp.where(owners[:, :, None, None], log_norms[None], 0.0), axis=1)
-    log_norm = jnp.transpose(log_norm, (1, 0, 2)).reshape(ROWS)
-    return weighted, log_norm
 
 
 def solution(mesh):

time: 168 us -> 159 us (0.946)
  Pallas kernels: 34.1 us -> 29.3 us
  waiting for transfers between devices: 50.8 us -> 48.7 us
    pallas_call x2 -> x3, Pallas kernels: 15.1 us -> 11.1 us  [the longest x1 4.44 us: weighted_sums(): pl.pallas_call(send_kernel, out_shape=(half, jax.ShapeDtypeStruct((1, COL...]
    ppermute x3, waiting for transfers between devices: 1.72 us -> 0.01 us  [shards(): lax.ppermute(scale, 'shell', to)]
    unnamed x39 -> x15, local copies, waits for them, and re-layouts: 5.75 us -> 5.12 us
  transfers between devices with their start and end apart: 35 -> 35, of which waited for: 15 -> 14; matrix products, arithmetic and copies ran while one was open for 3% -> 2% of each run, Pallas kernels for 13% -> 13%
where the time goes in v1:
time: 159 us
  starting transfers between devices  70.8 us (45%)
  waiting for transfers between devices  48.7 us (31%)
  Pallas kernels  29.3 us (18%)
  local copies, waits for them, and re-layouts  6.27 us (4%)
  other arithmetic  2.46 us (2%)
    ppermute x22, starting transfers between devices, step(): lax.ppermute(value, axis, [(i, (i + by) % count) for i in range(count)])  33.4 us
    ppermute x22, waiting for transfers between devices, step(): lax.ppermute(value, axis, [(i, (i + by) % count) for i in range(count)])  24.1 us
    ppermute x1, starting transfers between devices, weighted_sums(): other = lax.ppermute(out, 'dom', [(0, 1), (1, 0)])  17.7 us
    pallas_call x2, Pallas kernels, partial_scores(): pl.pallas_call(lambda *refs_: scores_kernel(order, k, *refs_), out_shape=...  11.1 us
    ppermute x2, waiting for transfers between devices, summed(): got = lax.ppermute(send, 'shell', first)  10.7 us
    all_to_all x1, starting transfers between devices, shards(): everyone = lax.all_to_all(stats, ('z', 'x'), 0, 0, tiled=True)  7.21 us
    ppermute x2, waiting for transfers between devices, summed(): last = lax.ppermute(keep1 + got[QUARTER:], 'shell', second)  6.87 us
    all_to_all x1, waiting for transfers between devices, shards(): everyone = lax.all_to_all(stats, ('z', 'x'), 0, 0, tiled=True)  5.33 us
  transfers between devices with their start and end apart: 35, of which 14 were waited for; matrix products, arithmetic and copies ran while one was open for 2% of the time, Pallas kernels for 13%

profile of v1, /device:TPU:1, one launch (start us, length us, event | category | flops | bytes accessed | tf_op | source)
XLA Modules:
  0.0 158.6 jit_solution(14198130368116922850)
XLA Ops:
  4.4 4.0 %collective-permute-start.6 = (bf16[32,2048]{1,0:T(8,128)(2,1)S(1)}, bf16[32,2048]{1,0:T(8,128)(2,1)S(1)}, u32[]{:S(2)}, u32[]{:S(2)}) collective-permute-start(bf16[32,2048]{1,0:T(8,128)(2,1)S(1)} %bitcast.17), channel_id=1, source_target_pairs={{0,224},{32,0},{64,32},{96,64},{128,96},{160,128},{192,160},{224,1... | collective-permute-start | bytes 393224 | tf_op jit(solution)/shard_map/ppermute | solution.py:34
  8.4 3.1 %collective-permute-done.3.rest_7_ = bf16[32,2048]{1,0:T(8,128)(2,1)S(1)} collective-permute-done((bf16[32,2048]{1,0:T(8,128)(2,1)S(1)}, bf16[32,2048]{1,0:T(8,128)(2,1)S(1)}, u32[]{:S(2)}, u32[]{:S(2)}) %collective-permute-start.3) | collective-permute-done | bytes 131104 | tf_op jit(solution)/shard_map/ppermute | solution.py:34
  16.5 2.7 %collective-permute-start.7 = (bf16[32,2048]{1,0:T(8,128)(2,1)S(1)}, bf16[32,2048]{1,0:T(8,128)(2,1)S(1)}, u32[]{:S(2)}, u32[]{:S(2)}) collective-permute-start(bf16[32,2048]{1,0:T(8,128)(2,1)S(1)} %collective-permute-done.6.rest_1_), channel_id=1, source_target_pairs={{0,224},{32,0},{64,32},{96,64},{128,96},{160,128},{192,160},{224,1... | collective-permute-start | bytes 393224 | tf_op jit(solution)/shard_map/ppermute | solution.py:34
  21.1 3.4 %collective-permute-start.8 = (bf16[32,2048]{1,0:T(8,128)(2,1)S(1)}, bf16[32,2048]{1,0:T(8,128)(2,1)S(1)}, u32[]{:S(2)}, u32[]{:S(2)}) collective-permute-start(bf16[32,2048]{1,0:T(8,128)(2,1)S(1)} %collective-permute-done.7.rest_2_), channel_id=1, source_target_pairs={{0,224},{32,0},{64,32},{96,64},{128,96},{160,128},{192,160},{224,1... | collective-permute-start | bytes 393224 | tf_op jit(solution)/shard_map/ppermute | solution.py:34
  26.4 3.1 %collective-permute-start.10 = (bf16[128,2048]{1,0:T(8,128)(2,1)S(1)}, bf16[128,2048]{1,0:T(8,128)(2,1)S(1)}, u32[]{:S(2)}, u32[]{:S(2)}) collective-permute-start(bf16[128,2048]{1,0:T(8,128)(2,1)S(1)} %joined.2.refs__4_), channel_id=1, source_target_pairs={{0,224},{32,0},{64,32},{96,64},{128,96},{160,128},{192,160},{224,1... | collective-permute-start | bytes 1572872 | tf_op jit(solution)/shard_map/ppermute | solution.py:34
  33.3 3.1 %collective-permute-done.10.refs__6_ = bf16[128,2048]{1,0:T(8,128)(2,1)S(1)} collective-permute-done((bf16[128,2048]{1,0:T(8,128)(2,1)S(1)}, bf16[128,2048]{1,0:T(8,128)(2,1)S(1)}, u32[]{:S(2)}, u32[]{:S(2)}) %collective-permute-start.10) | collective-permute-done | bytes 524320 | tf_op jit(solution)/shard_map/ppermute | solution.py:34
  36.4 3.7 %collective-permute-done.9.refs__5_ = bf16[128,2048]{1,0:T(8,128)(2,1)S(1)} collective-permute-done((bf16[128,2048]{1,0:T(8,128)(2,1)S(1)}, bf16[128,2048]{1,0:T(8,128)(2,1)S(1)}, u32[]{:S(2)}, u32[]{:S(2)}) %collective-permute-start.9) | collective-permute-done | bytes 524320 | tf_op jit(solution)/shard_map/ppermute | solution.py:34
  40.1 2.7 %collective-permute-start.12 = (bf16[128,2048]{1,0:T(8,128)(2,1)S(1)}, bf16[128,2048]{1,0:T(8,128)(2,1)S(1)}, u32[]{:S(2)}, u32[]{:S(2)}) collective-permute-start(bf16[128,2048]{1,0:T(8,128)(2,1)S(1)} %collective-permute-done.10.refs__6_), channel_id=1, source_target_pairs={{0,224},{32,0},{64,32},{96,64},{128,96},{160,128},{192,160},{224,1... | collective-permute-start | bytes 1572872 | tf_op jit(solution)/shard_map/ppermute | solution.py:34
  43.4 7.1 %collective-permute-done.11.refs__7_ = bf16[128,2048]{1,0:T(8,128)(2,1)S(1)} collective-permute-done((bf16[128,2048]{1,0:T(8,128)(2,1)S(1)}, bf16[128,2048]{1,0:T(8,128)(2,1)S(1)}, u32[]{:S(2)}, u32[]{:S(2)}) %collective-permute-start.11) | collective-permute-done | bytes 524320 | tf_op jit(solution)/shard_map/ppermute | solution.py:34
  50.6 2.7 %collective-permute-start.14 = (bf16[128,2048]{1,0:T(8,128)(2,1)S(1)}, bf16[128,2048]{1,0:T(8,128)(2,1)S(1)}, u32[]{:S(2)}, u32[]{:S(2)}) collective-permute-start(bf16[128,2048]{1,0:T(8,128)(2,1)S(1)} %collective-permute-done.12.refs__8_), channel_id=1, source_target_pairs={{0,224},{32,0},{64,32},{96,64},{128,96},{160,128},{192,160},{224,1... | collective-permute-start | bytes 1572872 | tf_op jit(solution)/shard_map/ppermute | solution.py:34
  56.1 5.4 %collective-permute-done.13.first.refs__9_ = bf16[128,2048]{1,0:T(8,128)(2,1)S(1)} collective-permute-done((bf16[128,2048]{1,0:T(8,128)(2,1)S(1)}, bf16[128,2048]{1,0:T(8,128)(2,1)S(1)}, u32[]{:S(2)}, u32[]{:S(2)}) %collective-permute-start.13) | collective-permute-done | bytes 524320 | tf_op jit(solution)/shard_map/ppermute | solution.py:34
  61.7 3.0 %collective-permute-start.16 = (bf16[64,2048]{1,0:T(8,128)(2,1)S(1)}, bf16[64,2048]{1,0:T(8,128)(2,1)S(1)}, u32[]{:S(2)}, u32[]{:S(2)}) collective-permute-start(bf16[64,2048]{1,0:T(8,128)(2,1)S(1)} %get-tuple-element.43), channel_id=1, source_target_pairs={{0,224},{32,0},{64,32},{96,64},{128,96},{160,128},{192,160},{224,1... | collective-permute-start | bytes 786440 | tf_op jit(solution)/shard_map/ppermute | solution.py:34
  64.7 5.6 %partial_scores.3 = (f32[384,512]{1,0:T(8,128)S(1)}, f32[192,512]{1,0:T(8,128)S(1)}, f32[192,512]{1,0:T(8,128)S(1)}, bf16[1024,2048]{1,0:T(8,128)(2,1)}) custom-call(s32[143]{0:T(256)S(1)} %compare_select_fusion.23.refs__0_.tab, bf16[512,2048]{1,0:T(8,128)(2,1)S(1)} %bitcast.14, f32[1,2048]{1,0:T(1,128)S(1)} %bitcast.23, f32[1,512]{1,0:T(1,128)S(1)} %bitcast.25, ...), custom_call_target="tpu_custom_call" | custom-call | flops 2147483648 | bytes 8388608 | tf_op jit(solution)/shard_map/partial_scores/pallas_call | solution.py:183
  70.3 2.8 %collective-permute-start.24 = (f32[384,512]{1,0:T(8,128)S(1)}, f32[384,512]{1,0:T(8,128)S(1)}, u32[]{:S(2)}, u32[]{:S(2)}) collective-permute-start(f32[384,512]{1,0:T(8,128)S(1)} %get-tuple-element.52), channel_id=1, source_target_pairs={{0,3},{3,0},{1,2},{2,1},{4,7},{7,4},{5,6},{6,5},{8,11},{11,8},{9,1... | collective-permute-start | bytes 2359304 | tf_op jit(solution)/shard_map/ppermute | solution.py:481
  73.1 5.6 %partial_scores.2 = (f32[384,512]{1,0:T(8,128)S(1)}, f32[192,512]{1,0:T(8,128)S(1)}, f32[192,512]{1,0:T(8,128)S(1)}, bf16[1024,2048]{1,0:T(8,128)(2,1)}) custom-call(s32[143]{0:T(256)S(1)} %compare_select_fusion.23.refs__0_.tab, bf16[512,2048]{1,0:T(8,128)(2,1)S(1)} %bitcast.15, f32[1,2048]{1,0:T(1,128)S(1)} %bitcast.24, f32[1,512]{1,0:T(1,128)S(1)} %bitcast.26, ...), custom_call_target="tpu_custom_call" | custom-call | flops 2147483648 | bytes 8388608 | tf_op jit(solution)/shard_map/partial_scores/pallas_call | solution.py:183
  78.8 3.7 %collective-permute-done.24.b1 = f32[384,512]{1,0:T(8,128)S(1)} collective-permute-done((f32[384,512]{1,0:T(8,128)S(1)}, f32[384,512]{1,0:T(8,128)S(1)}, u32[]{:S(2)}, u32[]{:S(2)}) %collective-permute-start.24) | collective-permute-done | bytes 786464 | tf_op jit(solution)/shard_map/ppermute | solution.py:481
  82.9 7.0 %collective-permute-done.17.a1 = f32[384,512]{1,0:T(8,128)S(1)} collective-permute-done((f32[384,512]{1,0:T(8,128)S(1)}, f32[384,512]{1,0:T(8,128)S(1)}, u32[]{:S(2)}, u32[]{:S(2)}) %collective-permute-start.17) | collective-permute-done | bytes 786464 | tf_op jit(solution)/shard_map/ppermute | solution.py:481
  91.0 4.5 %collective-permute-done.25.b2 = f32[192,512]{1,0:T(8,128)S(1)} collective-permute-done((f32[192,512]{1,0:T(8,128)S(1)}, f32[192,512]{1,0:T(8,128)S(1)}, u32[]{:S(2)}, u32[]{:S(2)}) %collective-permute-start.25) | collective-permute-done | bytes 393248 | tf_op jit(solution)/shard_map/ppermute | solution.py:482
  102.1 7.2 %all-to-all-start = ((f32[32,8,128]{2,1,0:T(8,128)}), f32[32,8,128]{2,1,0:T(8,128)S(1)}, u32[]{:S(2)}, u32[]{:S(2)}) async-start(f32[32,8,128]{2,1,0:T(8,128)} %get-tuple-element.54.own), calls=%async_computation | async-start | bytes 262144 | tf_op jit(solution)/shard_map/all_to_all | solution.py:495
  113.3 5.3 %all-to-all-done.everyone = f32[32,8,128]{2,1,0:T(8,128)S(1)} async-done(((f32[32,8,128]{2,1,0:T(8,128)}), f32[32,8,128]{2,1,0:T(8,128)S(1)}, u32[]{:S(2)}, u32[]{:S(2)}) %all-to-all-start) | async-done | bytes 131104 | tf_op jit(solution)/shard_map/all_to_all | solution.py:495
  127.4 3.0 %lay_posteriors.1 = (bf16[512,2048]{1,0:T(8,128)(2,1)S(1)}, bf16[2048,2048]{1,0:T(8,128)(2,1)S(1)}) custom-call(s32[143]{0:T(256)S(1)} %compare_select_fusion.23.refs__0_.tab, bf16[384,512]{1,0:T(8,128)(2,1)S(1)} %get-tuple-element.55.own, bf16[384,512]{1,0:T(8,128)(2,1)S(1)} %collective-permute-done.29.first.far, ...), custom_call_target="tpu_custom_call" | custom-call | tf_op jit(solution)/shard_map/lay_posteriors/pallas_call | solution.py:381
  130.4 4.4 %weighted_send.1 = (f32[256,2048]{1,0:T(8,128)S(1)}, f32[1,2048]{1,0:T(1,128)S(1)}) custom-call(s32[143]{0:T(256)S(1)} %compare_select_fusion.23.refs__0_.tab, f32[8,128]{1,0:T(8,128)S(1)} %combine_stats.1.rest_0_, f32[8,128]{1,0:T(8,128)S(1)} %collective-permute-done.26.rest_1_, f32[8,128]{1,0:T(8,128)S(1)} %collective-permute-done.27.rest_2_, ...), custom_call_target="tpu_custom_call" | custom-call | flops 2147483648 | bytes 12582912 | tf_op jit(solution)/shard_map/weighted_send/pallas_call | solution.py:397
  134.8 17.7 %collective-permute-start.33 = (f32[256,2048]{1,0:T(8,128)S(1)}, f32[256,2048]{1,0:T(8,128)S(1)}, u32[]{:S(2)}, u32[]{:S(2)}) collective-permute-start(f32[256,2048]{1,0:T(8,128)S(1)} %get-tuple-element.64), channel_id=1, source_target_pairs={{0,4},{4,0},{1,5},{5,1},{2,6},{6,2},{3,7},{7,3},{8,12},{12,8},{9,1... | collective-permute-start | bytes 6291464 | tf_op jit(solution)/shard_map/ppermute | solution.py:413
  152.5 3.6 %weighted_keep.1 = (f32[256,2048]{1,0:T(8,128)S(1)}, f32[1,64]{1,0:T(1,128)}) custom-call(s32[143]{0:T(256)S(1)} %compare_select_fusion.23.refs__0_.tab, f32[8,128]{1,0:T(8,128)S(1)} %combine_stats.1.rest_0_, f32[8,128]{1,0:T(8,128)S(1)} %collective-permute-done.26.rest_1_, f32[8,128]{1,0:T(8,128)S(1)} %collective-permute-done.27.rest_2_, ...), custom_call_target="tpu_custom_call" | custom-call | flops 2147483648 | bytes 12582912 | tf_op jit(solution)/shard_map/weighted_keep/pallas_call | solution.py:414
  (85 shorter events, 42.9 us)
Async XLA Ops:
  4.4 12.1 %collective-permute-start.6 = (bf16[32,2048]{1,0:T(8,128)(2,1)S(1)}, bf16[32,2048]{1,0:T(8,128)(2,1)S(1)}, u32[]{:S(2)}, u32[]{:S(2)}) collective-permute-start(bf16[32,2048]{1,0:T(8,128)(2,1)S(1)} %bitcast.17), channel_id=1, source_target_pairs={{0,224},{32,0},{64,32},{96,64},{128,96},{160,128},{192,160},{224,1... | collective-permute-start | bytes 393224 | tf_op jit(solution)/shard_map/ppermute | solution.py:34
  11.6 12.9 %collective-permute-start.2 = (bf16[32,2048]{1,0:T(8,128)(2,1)S(1)}, bf16[32,2048]{1,0:T(8,128)(2,1)S(1)}, u32[]{:S(2)}, u32[]{:S(2)}) collective-permute-start(bf16[32,2048]{1,0:T(8,128)(2,1)S(1)} %bitcast.19), channel_id=1, source_target_pairs={{0,8},{8,16},{16,24},{24,0},{1,9},{9,17},{17,25},{25,1},{2,10},{10... | collective-permute-start | bytes 393224 | tf_op jit(solution)/shard_map/ppermute | solution.py:34
  12.8 11.6 %collective-permute-start.1 = (bf16[32,2048]{1,0:T(8,128)(2,1)S(1)}, bf16[32,2048]{1,0:T(8,128)(2,1)S(1)}, u32[]{:S(2)}, u32[]{:S(2)}) collective-permute-start(bf16[32,2048]{1,0:T(8,128)(2,1)S(1)} %bitcast.20), channel_id=1, source_target_pairs={{0,16},{8,24},{16,0},{24,8},{1,17},{9,25},{17,1},{25,9},{2,18},{10... | collective-permute-start | bytes 393224 | tf_op jit(solution)/shard_map/ppermute | solution.py:34
  29.5 10.6 %collective-permute-start.9 = (bf16[128,2048]{1,0:T(8,128)(2,1)S(1)}, bf16[128,2048]{1,0:T(8,128)(2,1)S(1)}, u32[]{:S(2)}, u32[]{:S(2)}) collective-permute-start(bf16[128,2048]{1,0:T(8,128)(2,1)S(1)} %joined.2.refs__4_), channel_id=1, source_target_pairs={{0,32},{32,64},{64,96},{96,128},{128,160},{160,192},{192,224},{224... | collective-permute-start | bytes 1572872 | tf_op jit(solution)/shard_map/ppermute | solution.py:34
  30.9 22.3 %collective-permute-start.21 = (bf16[256,2048]{1,0:T(8,128)(2,1)S(1)}, bf16[256,2048]{1,0:T(8,128)(2,1)S(1)}, u32[]{:S(2)}, u32[]{:S(2)}) collective-permute-start(bf16[256,2048]{1,0:T(8,128)(2,1)S(1)} %joined.3.refs__4_), channel_id=1, source_target_pairs={{0,24},{8,0},{16,8},{24,16},{1,25},{9,1},{17,9},{25,17},{2,26},{10... | collective-permute-start | bytes 3145736 | tf_op jit(solution)/shard_map/ppermute | solution.py:34
  31.0 22.3 %collective-permute-start.20 = (bf16[256,2048]{1,0:T(8,128)(2,1)S(1)}, bf16[256,2048]{1,0:T(8,128)(2,1)S(1)}, u32[]{:S(2)}, u32[]{:S(2)}) collective-permute-start(bf16[256,2048]{1,0:T(8,128)(2,1)S(1)} %joined.3.refs__4_), channel_id=1, source_target_pairs={{0,8},{8,16},{16,24},{24,0},{1,9},{9,17},{17,25},{25,1},{2,10},{10... | collective-permute-start | bytes 3145736 | tf_op jit(solution)/shard_map/ppermute | solution.py:34
  40.1 10.5 %collective-permute-start.11 = (bf16[128,2048]{1,0:T(8,128)(2,1)S(1)}, bf16[128,2048]{1,0:T(8,128)(2,1)S(1)}, u32[]{:S(2)}, u32[]{:S(2)}) collective-permute-start(bf16[128,2048]{1,0:T(8,128)(2,1)S(1)} %collective-permute-done.9.refs__5_), channel_id=1, source_target_pairs={{0,32},{32,64},{64,96},{96,128},{128,160},{160,192},{192,224},{224... | collective-permute-start | bytes 1572872 | tf_op jit(solution)/shard_map/ppermute | solution.py:34
  40.1 10.5 %collective-permute-start.12 = (bf16[128,2048]{1,0:T(8,128)(2,1)S(1)}, bf16[128,2048]{1,0:T(8,128)(2,1)S(1)}, u32[]{:S(2)}, u32[]{:S(2)}) collective-permute-start(bf16[128,2048]{1,0:T(8,128)(2,1)S(1)} %collective-permute-done.10.refs__6_), channel_id=1, source_target_pairs={{0,224},{32,0},{64,32},{96,64},{128,96},{160,128},{192,160},{224,1... | collective-permute-start | bytes 1572872 | tf_op jit(solution)/shard_map/ppermute | solution.py:34
  50.6 10.9 %collective-permute-start.13 = (bf16[128,2048]{1,0:T(8,128)(2,1)S(1)}, bf16[128,2048]{1,0:T(8,128)(2,1)S(1)}, u32[]{:S(2)}, u32[]{:S(2)}) collective-permute-start(bf16[128,2048]{1,0:T(8,128)(2,1)S(1)} %collective-permute-done.11.refs__7_), channel_id=1, source_target_pairs={{0,32},{32,64},{64,96},{96,128},{128,160},{160,192},{192,224},{224... | collective-permute-start | bytes 1572872 | tf_op jit(solution)/shard_map/ppermute | solution.py:34
  50.6 10.9 %collective-permute-start.14 = (bf16[128,2048]{1,0:T(8,128)(2,1)S(1)}, bf16[128,2048]{1,0:T(8,128)(2,1)S(1)}, u32[]{:S(2)}, u32[]{:S(2)}) collective-permute-start(bf16[128,2048]{1,0:T(8,128)(2,1)S(1)} %collective-permute-done.12.refs__8_), channel_id=1, source_target_pairs={{0,224},{32,0},{64,32},{96,64},{128,96},{160,128},{192,160},{224,1... | collective-permute-start | bytes 1572872 | tf_op jit(solution)/shard_map/ppermute | solution.py:34
  53.3 11.4 %collective-permute-start.22 = (bf16[128,2048]{1,0:T(8,128)(2,1)S(1)}, bf16[128,2048]{1,0:T(8,128)(2,1)S(1)}, u32[]{:S(2)}, u32[]{:S(2)}) collective-permute-start(bf16[128,2048]{1,0:T(8,128)(2,1)S(1)} %get-tuple-element.49), channel_id=1, source_target_pairs={{0,8},{8,16},{16,24},{24,0},{1,9},{9,17},{17,25},{25,1},{2,10},{10... | collective-permute-start | bytes 1572872 | tf_op jit(solution)/shard_map/ppermute | solution.py:34
  53.4 11.3 %collective-permute-start.23 = (bf16[128,2048]{1,0:T(8,128)(2,1)S(1)}, bf16[128,2048]{1,0:T(8,128)(2,1)S(1)}, u32[]{:S(2)}, u32[]{:S(2)}) collective-permute-start(bf16[128,2048]{1,0:T(8,128)(2,1)S(1)} %get-tuple-element.50), channel_id=1, source_target_pairs={{0,24},{8,0},{16,8},{24,16},{1,25},{9,1},{17,9},{25,17},{2,26},{10... | collective-permute-start | bytes 1572872 | tf_op jit(solution)/shard_map/ppermute | solution.py:34
  61.6 11.5 %collective-permute-start.15 = (bf16[64,2048]{1,0:T(8,128)(2,1)S(1)}, bf16[64,2048]{1,0:T(8,128)(2,1)S(1)}, u32[]{:S(2)}, u32[]{:S(2)}) collective-permute-start(bf16[64,2048]{1,0:T(8,128)(2,1)S(1)} %get-tuple-element.42), channel_id=1, source_target_pairs={{0,32},{32,64},{64,96},{96,128},{128,160},{160,192},{192,224},{224... | collective-permute-start | bytes 786440 | tf_op jit(solution)/shard_map/ppermute | solution.py:34
  61.7 11.4 %collective-permute-start.16 = (bf16[64,2048]{1,0:T(8,128)(2,1)S(1)}, bf16[64,2048]{1,0:T(8,128)(2,1)S(1)}, u32[]{:S(2)}, u32[]{:S(2)}) collective-permute-start(bf16[64,2048]{1,0:T(8,128)(2,1)S(1)} %get-tuple-element.43), channel_id=1, source_target_pairs={{0,224},{32,0},{64,32},{96,64},{128,96},{160,128},{192,160},{224,1... | collective-permute-start | bytes 786440 | tf_op jit(solution)/shard_map/ppermute | solution.py:34
  70.3 12.2 %collective-permute-start.24 = (f32[384,512]{1,0:T(8,128)S(1)}, f32[384,512]{1,0:T(8,128)S(1)}, u32[]{:S(2)}, u32[]{:S(2)}) collective-permute-start(f32[384,512]{1,0:T(8,128)S(1)} %get-tuple-element.52), channel_id=1, source_target_pairs={{0,3},{3,0},{1,2},{2,1},{4,7},{7,4},{5,6},{6,5},{8,11},{11,8},{9,1... | collective-permute-start | bytes 2359304 | tf_op jit(solution)/shard_map/ppermute | solution.py:481
  78.7 11.2 %collective-permute-start.17 = (f32[384,512]{1,0:T(8,128)S(1)}, f32[384,512]{1,0:T(8,128)S(1)}, u32[]{:S(2)}, u32[]{:S(2)}) collective-permute-start(f32[384,512]{1,0:T(8,128)S(1)} %get-tuple-element.45), channel_id=1, source_target_pairs={{0,1},{1,0},{2,3},{3,2},{4,5},{5,4},{6,7},{7,6},{8,9},{9,8},{10,11... | collective-permute-start | bytes 2359304 | tf_op jit(solution)/shard_map/ppermute | solution.py:481
  82.5 13.1 %collective-permute-start.25 = (f32[192,512]{1,0:T(8,128)S(1)}, f32[192,512]{1,0:T(8,128)S(1)}, u32[]{:S(2)}, u32[]{:S(2)}) collective-permute-start(f32[192,512]{1,0:T(8,128)S(1)} %slice_add_fusion), channel_id=1, source_target_pairs={{0,1},{1,0},{2,3},{3,2},{4,5},{5,4},{6,7},{7,6},{8,9},{9,8},{10,11... | collective-permute-start | bytes 1179656 | tf_op jit(solution)/shard_map/ppermute | solution.py:482
  99.7 11.2 %collective-permute-start.30 = (bf16[384,512]{1,0:T(8,128)(2,1)S(1)}, bf16[384,512]{1,0:T(8,128)(2,1)S(1)}, u32[]{:S(2)}, u32[]{:S(2)}) collective-permute-start(bf16[384,512]{1,0:T(8,128)(2,1)S(1)} %get-tuple-element.55.own), channel_id=1, source_target_pairs={{0,1},{1,0},{2,3},{3,2},{4,5},{5,4},{6,7},{7,6},{8,9},{9,8},{10,11... | collective-permute-start | bytes 1179656 | tf_op jit(solution)/shard_map/ppermute | solution.py:490
  99.7 11.2 %collective-permute-start.29 = (bf16[384,512]{1,0:T(8,128)(2,1)S(1)}, bf16[384,512]{1,0:T(8,128)(2,1)S(1)}, u32[]{:S(2)}, u32[]{:S(2)}) collective-permute-start(bf16[384,512]{1,0:T(8,128)(2,1)S(1)} %get-tuple-element.55.own), channel_id=1, source_target_pairs={{0,3},{3,0},{1,2},{2,1},{4,7},{7,4},{5,6},{6,5},{8,11},{11,8},{9,1... | collective-permute-start | bytes 1179656 | tf_op jit(solution)/shard_map/ppermute | solution.py:491
  102.1 16.6 %all-to-all-start = ((f32[32,8,128]{2,1,0:T(8,128)}), f32[32,8,128]{2,1,0:T(8,128)S(1)}, u32[]{:S(2)}, u32[]{:S(2)}) async-start(f32[32,8,128]{2,1,0:T(8,128)} %get-tuple-element.54.own), calls=%async_computation | async-start | bytes 262144 | tf_op jit(solution)/shard_map/all_to_all | solution.py:495
  110.9 12.0 %collective-permute-start.31 = (bf16[192,512]{1,0:T(8,128)(2,1)S(1)}, bf16[192,512]{1,0:T(8,128)(2,1)S(1)}, u32[]{:S(2)}, u32[]{:S(2)}) collective-permute-start(bf16[192,512]{1,0:T(8,128)(2,1)S(1)} %get-tuple-element.56), channel_id=1, source_target_pairs={{0,1},{1,0},{2,3},{3,2},{4,5},{5,4},{6,7},{7,6},{8,9},{9,8},{10,11... | collective-permute-start | bytes 589832 | tf_op jit(solution)/shard_map/ppermute | solution.py:493
  111.1 11.9 %collective-permute-start.32 = (bf16[192,512]{1,0:T(8,128)(2,1)S(1)}, bf16[192,512]{1,0:T(8,128)(2,1)S(1)}, u32[]{:S(2)}, u32[]{:S(2)}) collective-permute-start(bf16[192,512]{1,0:T(8,128)(2,1)S(1)} %get-tuple-element.57), channel_id=1, source_target_pairs={{0,3},{3,0},{1,2},{2,1},{4,7},{7,4},{5,6},{6,5},{8,11},{11,8},{9,1... | collective-permute-start | bytes 589832 | tf_op jit(solution)/shard_map/ppermute | solution.py:494
  119.6 10.7 %collective-permute-start.28 = (f32[8,128]{1,0:T(8,128)S(1)}, f32[8,128]{1,0:T(8,128)S(1)}, u32[]{:S(2)}, u32[]{:S(2)}) collective-permute-start(f32[8,128]{1,0:T(8,128)S(1)} %combine_stats.1.rest_0_), channel_id=1, source_target_pairs={{0,2},{2,0},{1,3},{3,1},{4,6},{6,4},{5,7},{7,5},{8,10},{10,8},{9,1... | collective-permute-start | bytes 12296 | tf_op jit(solution)/shard_map/ppermute | solution.py:499
  134.8 21.5 %collective-permute-start.33 = (f32[256,2048]{1,0:T(8,128)S(1)}, f32[256,2048]{1,0:T(8,128)S(1)}, u32[]{:S(2)}, u32[]{:S(2)}) collective-permute-start(f32[256,2048]{1,0:T(8,128)S(1)} %get-tuple-element.64), channel_id=1, source_target_pairs={{0,4},{4,0},{1,5},{5,1},{2,6},{6,2},{3,7},{7,3},{8,12},{12,8},{9,1... | collective-permute-start | bytes 6291464 | tf_op jit(solution)/shard_map/ppermute | solution.py:413
  (17 other events, 121.3 us)

commit v2 on v1

--- a/solution.py
+++ b/solution.py
@@ -92,7 +92,7 @@
     return step(up, axis, count, 1), step(down, axis, count, -1)
 
 
-def gather(half_a, half_b, flat, norm_of, tab):
+def gather(half_a, half_b, flat, norm_of, weight, tab):
     downs, ups = [half_b], [half_b]
     down, up = both_ways(half_b, half_b, "z", NZ)
     low, high = both_ways(half_a, half_a, "x", NX)
@@ -118,19 +118,15 @@
     down, up, norm = lax.optimization_barrier((down, up, norm))
     far_b = both_ways(*halves(low, high), "x", NX)
     down, up = both_ways(down, up, "z", NZ)
-    pieces_a += [down, up]
-    pieces_a += both_ways(*halves(down, up), "z", NZ)
-    return pieces_a, [mine_b, low, high, *far_b], flat, norm, tab
-
-
-def scores_kernel(order, k, tab, refs, weight, norm, *rest):
-    arrays = rest[: len(order)]
-    outs, (images, parts, whole, scaled, held, near_refs, sems) = (
-        rest[len(order) : len(order) + 3],
-        rest[len(order) + 3 :],
-    )
+    early, images = early_scores(flat, weight, norm, pieces_a)
+    early, down, up = lax.optimization_barrier((early, down, up))
+    pieces_a = [down, up, *both_ways(*halves(down, up), "z", NZ)]
+    return early, images, pieces_a, [mine_b, low, high, *far_b], flat, norm, tab
+
+
+def scaled_product(arrays, refs, weight, norm, whole, scaled, near_refs, images, sems):
     copies = fetch(arrays, whole, sems)
-    [(refs_copy, _, _)] = fetch([refs], near_refs, sems, len(order))
+    [(refs_copy, _, _)] = fetch([refs], near_refs, sems, len(arrays))
     for copy, base, count in copies:
         copy.wait()
 
@@ -142,18 +138,68 @@
             return carry
 
         lax.fori_loop(0, count // 16, tile, 0)
-    images_write = pltpu.make_async_copy(whole, images, sems.at[len(order) + 4])
+    images_write = pltpu.make_async_copy(whole, images, sems.at[len(arrays) + 1])
     images_write.start()
     refs_copy.wait()
-    held[...] = (
-        lax.dot_general(
-            scaled[...],
-            near_refs[...],
-            (((1,), (1,)), ((), ())),
-            preferred_element_type=jnp.float32,
+    value = lax.dot_general(
+        scaled[...],
+        near_refs[...],
+        (((1,), (1,)), ((), ())),
+        preferred_element_type=jnp.float32,
+    )
+    return value - norm[...], images_write
+
+
+def early_kernel(refs, weight, norm, *rest):
+    arrays, (out, images, held, whole, scaled, near_refs, sems) = rest[:-7], rest[-7:]
+    held[...], images_write = scaled_product(
+        arrays, refs, weight, norm, whole, scaled, near_refs, images, sems
+    )
+    write = pltpu.make_async_copy(held, out, sems.at[len(arrays) + 2])
+    write.start()
+    write.wait()
+    images_write.wait()
+
+
+def early_scores(refs, weight, norm, pieces):
+    rows = sum(p.shape[0] for p in pieces)
+    return pl.pallas_call(
+        early_kernel,
+        out_shape=(
+            jax.ShapeDtypeStruct((rows, REFS), jnp.float32),
+            jax.ShapeDtypeStruct((rows, COLS), jnp.bfloat16),
+        ),
+        in_specs=[ANY, VMEM, VMEM] + [ANY] * len(pieces),
+        out_specs=(ANY, ANY),
+        scratch_shapes=[
+            pltpu.VMEM((rows, REFS), jnp.float32),
+            pltpu.VMEM((rows, COLS), jnp.bfloat16),
+            pltpu.VMEM((rows, COLS), jnp.bfloat16),
+            pltpu.VMEM((REFS, COLS), jnp.bfloat16),
+            pltpu.SemaphoreType.DMA((len(pieces) + 3,)),
+        ],
+        compiler_params=pltpu.CompilerParams(vmem_limit_bytes=44 << 20),
+        cost_estimate=pl.CostEstimate(
+            flops=2 * rows * COLS * REFS, bytes_accessed=8 << 20, transcendentals=0
+        ),
+        name="early_scores",
+    )(refs, weight, norm, *pieces)
+
+
+def scores_kernel(k, pieces, first, tab, refs, weight, norm, *rest):
+    early, arrays, rest = rest[: first > 0], rest[first > 0 :][:pieces], rest[first > 0 :][pieces:]
+    outs, (images, parts, whole, scaled, held, near_refs, sems) = rest[:3], rest[3:]
+    if early:
+        early_copy = pltpu.make_async_copy(
+            early[0], held.at[pl.ds(0, first), :], sems.at[pieces + 2]
         )
-        - norm[...]
-    )
+        early_copy.start()
+    held[first:, :], images_write = scaled_product(
+        arrays, refs, weight, norm, whole, scaled, near_refs, images, sems
+    )
+    if early:
+        early_copy.wait()
+
     def compact(n, carry):
         slot = tab[k * BLOCKS + n]
 
@@ -170,35 +216,36 @@
     done = []
     for i, (out, t, count) in enumerate(zip(outs, (2, 0, 1), (2, 1, 1))):
         source = parts.at[pl.ds(t * QUARTER, count * QUARTER), :]
-        done.append(pltpu.make_async_copy(source, out, sems.at[len(order) + 1 + i]))
+        done.append(pltpu.make_async_copy(source, out, sems.at[pieces + 3 + i]))
         done[-1].start()
     for copy in done:
         copy.wait()
     images_write.wait()
 
 
-def partial_scores(order, k, tab, refs, weight, norm, pieces):
+def partial_scores(k, tab, refs, weight, norm, pieces, early=()):
     part = jax.ShapeDtypeStruct((QUARTER, REFS), jnp.float32)
     both = jax.ShapeDtypeStruct((2 * QUARTER, REFS), jnp.float32)
+    rows = sum(p.shape[0] for p in pieces)
     return pl.pallas_call(
-        lambda *refs_: scores_kernel(order, k, *refs_),
-        out_shape=(both, part, part, jax.ShapeDtypeStruct((1024, COLS), jnp.bfloat16)),
-        in_specs=[SMEM, ANY, VMEM, VMEM] + [ANY] * len(pieces),
+        lambda *refs_: scores_kernel(k, len(pieces), 1024 - rows, *refs_),
+        out_shape=(both, part, part, jax.ShapeDtypeStruct((rows, COLS), jnp.bfloat16)),
+        in_specs=[SMEM, ANY, VMEM, VMEM] + [ANY] * (len(early) + len(pieces)),
         out_specs=(ANY, ANY, ANY, ANY),
         scratch_shapes=[
             pltpu.VMEM((NY * QUARTER, REFS), jnp.float32),
-            pltpu.VMEM((1024, COLS), jnp.bfloat16),
-            pltpu.VMEM((1024, COLS), jnp.bfloat16),
+            pltpu.VMEM((rows, COLS), jnp.bfloat16),
+            pltpu.VMEM((rows, COLS), jnp.bfloat16),
             pltpu.VMEM((1024, REFS), jnp.float32),
             pltpu.VMEM((REFS, COLS), jnp.bfloat16),
-            pltpu.SemaphoreType.DMA((len(pieces) + 5,)),
+            pltpu.SemaphoreType.DMA((len(pieces) + 6,)),
         ],
         compiler_params=pltpu.CompilerParams(vmem_limit_bytes=44 << 20),
         cost_estimate=pl.CostEstimate(
-            flops=2 * 1024 * COLS * REFS, bytes_accessed=8 << 20, transcendentals=0
+            flops=2 * rows * COLS * REFS, bytes_accessed=8 << 20, transcendentals=0
         ),
         name="partial_scores",
-    )(tab, refs, weight, norm, *pieces)
+    )(tab, refs, weight, norm, *early, *pieces)
 
 
 def diagonal():
@@ -273,8 +320,7 @@
     )(everyone, own)
 
 
-def lay_kernel(tab, own, far, near, top, low, first, second, flipped, images, dense, probs, sems):
-    copies = [copy for copy, _, _ in fetch((first, second), images, sems)]
+def lay_kernel(tab, own, far, near, top, low, flipped, dense, probs):
     cut = MOST * 8
     for i, source in enumerate((own, far, near)):
         probs[i] = source[...]
@@ -295,8 +341,18 @@
 
         lax.fori_loop(0, BLOCKS, fill, 0)
         flipped[:, 1024 * k : 1024 * k + 1024] = dense[...].T
-    for copy in copies:
-        copy.wait()
+
+
+def product(half, images):
+    total, at = None, 0
+    for piece in images:
+        rows = piece.shape[0]
+        value = jnp.dot(
+            half[:, at : at + rows], piece[...], preferred_element_type=jnp.float32
+        )
+        total = value if total is None else total + value
+        at += rows
+    return total
 
 
 def scaled_rows(flipped, factor, base, out):
@@ -310,7 +366,8 @@
 
 
 def send_kernel(tab, *rest):
-    scales, (flipped, images, out, factor, total, half, column, ordered, sem) = rest[:4], rest[4:]
+    scales, flipped, images, rest = rest[:4], rest[4], rest[5:8], rest[8:]
+    out, factor, total, half, column, ordered, sem = rest
     eye = diagonal()
     for q, scale in enumerate(scales):
         for g in range(4):
@@ -335,16 +392,17 @@
             jnp.where(eye, square, 0.0), axis=0, keepdims=True
         )
     scaled_rows(flipped, factor, tab[4 * BLOCKS], half)
-    total[...] = jnp.dot(half[...], images[...], preferred_element_type=jnp.float32)
+    total[...] = product(half, images)
     write = pltpu.make_async_copy(total, out, sem)
     write.start()
     write.wait()
 
 
 def keep_kernel(tab, *rest):
-    scales, (flipped, images, factor, out, norms, half) = rest[:4], rest[4:]
+    scales, flipped, images, rest = rest[:4], rest[4], rest[5:8], rest[8:]
+    factor, out, norms, half = rest
     scaled_rows(flipped, factor, tab[4 * BLOCKS + 1], half)
-    out[...] = jnp.dot(half[...], images[...], preferred_element_type=jnp.float32)
+    out[...] = product(half, images)
     home = tab[4 * BLOCKS + 14]
     lane = lax.broadcasted_iota(jnp.int32, (1, 128), 1)
     spot = home % 16
@@ -373,31 +431,30 @@
         out[rows, 1, :] = total[:, COLS // 2 :]
 
 
-def weighted_sums(tab, scales, probs, pieces):
+def weighted_sums(tab, scales, probs, images):
     half = jax.ShapeDtypeStruct((REFS // 2, COLS), jnp.float32)
     cost = pl.CostEstimate(
         flops=2 * 2048 * COLS * REFS // 2, bytes_accessed=12 << 20, transcendentals=0
     )
-    flipped, images = pl.pallas_call(
+    flipped = pl.pallas_call(
         lay_kernel,
-        out_shape=(
-            jax.ShapeDtypeStruct((REFS, COLS), jnp.bfloat16),
-            jax.ShapeDtypeStruct((2048, COLS), jnp.bfloat16),
-        ),
-        in_specs=[SMEM] + [VMEM] * 5 + [ANY] * 2,
-        out_specs=(VMEM, VMEM),
+        out_shape=jax.ShapeDtypeStruct((REFS, COLS), jnp.bfloat16),
+        in_specs=[SMEM] + [VMEM] * 5,
+        out_specs=VMEM,
         scratch_shapes=[
             pltpu.VMEM((1024, REFS), jnp.bfloat16),
             pltpu.VMEM((NY, MOST * 16, REFS), jnp.bfloat16),
-            pltpu.SemaphoreType.DMA((2,)),
         ],
         compiler_params=pltpu.CompilerParams(vmem_limit_bytes=16 << 20),
+        cost_estimate=pl.CostEstimate(
+            flops=0, bytes_accessed=16 << 20, transcendentals=0
+        ),
         name="lay_posteriors",
-    )(tab, *probs, *pieces)
+    )(tab, *probs)
     out, factor = pl.pallas_call(
         send_kernel,
         out_shape=(half, jax.ShapeDtypeStruct((1, COLS), jnp.float32)),
-        in_specs=[SMEM] + [VMEM] * 6,
+        in_specs=[SMEM] + [VMEM] * 8,
         out_specs=(ANY, VMEM),
         scratch_shapes=[
             pltpu.VMEM((REFS // 2, COLS), jnp.float32),
@@ -409,18 +466,18 @@
         compiler_params=pltpu.CompilerParams(vmem_limit_bytes=16 << 20),
         cost_estimate=cost,
         name="weighted_send",
-    )(tab, *scales, flipped, images)
+    )(tab, *scales, flipped, *images)
     other = lax.ppermute(out, "dom", [(0, 1), (1, 0)])
     mine, norms = pl.pallas_call(
         keep_kernel,
         out_shape=(half, jax.ShapeDtypeStruct((1, ROWS), jnp.float32)),
-        in_specs=[SMEM] + [VMEM] * 7,
+        in_specs=[SMEM] + [VMEM] * 9,
         out_specs=(VMEM, VMEM),
         scratch_shapes=[pltpu.VMEM((REFS // 2, COLS), jnp.bfloat16)],
         compiler_params=pltpu.CompilerParams(vmem_limit_bytes=16 << 20),
         cost_estimate=cost,
         name="weighted_keep",
-    )(tab, *scales, flipped, images, factor)
+    )(tab, *scales, flipped, *images, factor)
     weighted = pl.pallas_call(
         final_kernel,
         out_shape=jax.ShapeDtypeStruct((REFS // 2, 2, COLS // 2), jnp.float32),
@@ -471,19 +528,19 @@
     tab = jnp.where(index < 2 * BLOCKS, slot, jnp.where(index < 4 * BLOCKS, block, tab))
 
     img = images.reshape(ROWS, COLS)
-    pieces_a, pieces_b, refs, norm, tab = gather(
-        img[:HALF], img[HALF:], references.reshape(REFS, COLS), norm_of, tab
+    early, early_images, pieces_a, pieces_b, refs, norm, tab = gather(
+        img[:HALF], img[HALF:], references.reshape(REFS, COLS), norm_of, weight[None, :], tab
     )
     weight = weight[None, :]
 
-    def summed(order, k, pieces, first, second):
-        send, keep0, keep1, whole = partial_scores(order, k, tab, refs, weight, norm, pieces)
+    def summed(k, pieces, early, first, second):
+        send, keep0, keep1, whole = partial_scores(k, tab, refs, weight, norm, pieces, early)
         got = lax.ppermute(send, "shell", first)
         last = lax.ppermute(keep1 + got[QUARTER:], "shell", second)
         return (keep0, got, last), whole
 
-    sum_a, whole_a = summed(ORDER_A, 0, pieces_a, to_near, to_far)
-    sum_b, whole_b = summed(ORDER_B, 1, pieces_b, to_far, to_near)
+    sum_a, whole_a = summed(0, pieces_a, (early,), to_near, to_far)
+    sum_b, whole_b = summed(1, pieces_b, (), to_far, to_near)
 
     probs, stats = local_stats(kept, sum_a, sum_b)
 
@@ -501,7 +558,7 @@
         tab,
         scales,
         (probs, from_far, from_near, across_top, across_low),
-        (whole_a, whole_b),
+        (early_images, whole_a, whole_b),
     )
 
 

time: 159 us -> 157 us (0.987)
  waiting for transfers between devices: 48.7 us -> 46 us
  Pallas kernels: 29.3 us -> 31.4 us
  local copies, waits for them, and re-layouts: 6.27 us -> 4.23 us
    ppermute x22, waiting for transfers between devices: 24.1 us -> 21.4 us  [step(): lax.ppermute(value, axis, [(i, (i + by) % count) for i in range(count)])]
    unnamed x15 -> x17, local copies, waits for them, and re-layouts: 5.12 us -> 2.93 us
    ppermute x2, waiting for transfers between devices: 6.87 us -> 8.67 us  [summed(): last = lax.ppermute(keep1 + got[QUARTER:], 'shell', second)]
    ppermute x1, waiting for transfers between devices: 0.01 us -> 1.76 us  [shards(): from_far = lax.ppermute(probs, 'shell', to_far)]
    all_to_all x1, waiting for transfers between devices: 5.33 us -> 3.59 us  [shards(): everyone = lax.all_to_all(stats, ('z', 'x'), 0, 0, tiled=True)]
    pallas_call x3 -> x4, Pallas kernels: 14.1 us -> 14.8 us  [the longest x2 8.91 us: partial_scores(): pl.pallas_call(lambda *refs_: scores_kernel(k, len(pieces), 1024 - rows,...]
  transfers between devices with their start and end apart: 35 -> 35, of which waited for: 14 -> 13; matrix products, arithmetic and copies ran while one was open for 2% -> 2% of each run, Pallas kernels for 13% -> 15%
where the time goes in v2:
time: 157 us
  starting transfers between devices  71.9 us (46%)
  waiting for transfers between devices  46 us (29%)
  Pallas kernels  31.4 us (20%)
  local copies, waits for them, and re-layouts  4.23 us (3%)
  other arithmetic  2.33 us (1%)
    ppermute x22, starting transfers between devices, step(): lax.ppermute(value, axis, [(i, (i + by) % count) for i in range(count)])  33.4 us
    ppermute x22, waiting for transfers between devices, step(): lax.ppermute(value, axis, [(i, (i + by) % count) for i in range(count)])  21.4 us
    ppermute x1, starting transfers between devices, weighted_sums(): other = lax.ppermute(out, 'dom', [(0, 1), (1, 0)])  17.1 us
    ppermute x2, waiting for transfers between devices, summed(): got = lax.ppermute(send, 'shell', first)  10.6 us
    pallas_call x2, Pallas kernels, partial_scores(): pl.pallas_call(lambda *refs_: scores_kernel(k, len(pieces), 1024 - rows,...  8.91 us
    ppermute x2, waiting for transfers between devices, summed(): last = lax.ppermute(keep1 + got[QUARTER:], 'shell', second)  8.67 us
    all_to_all x1, starting transfers between devices, shards(): everyone = lax.all_to_all(stats, ('z', 'x'), 0, 0, tiled=True)  7.45 us
    pallas_call x1, Pallas kernels, weighted_sums(): pl.pallas_call(send_kernel, out_shape=(half, jax.ShapeDtypeStruct((1, COL...  4.7 us
  transfers between devices with their start and end apart: 35, of which 13 were waited for; matrix products, arithmetic and copies ran while one was open for 2% of the time, Pallas kernels for 15%

profile of v2, /device:TPU:1, one launch (start us, length us, event | category | flops | bytes accessed | tf_op | source)
XLA Modules:
  0.0 156.9 jit_solution(14805429964421293416)
XLA Ops:
  4.5 4.0 %collective-permute-start.6 = (bf16[32,2048]{1,0:T(8,128)(2,1)S(1)}, bf16[32,2048]{1,0:T(8,128)(2,1)S(1)}, u32[]{:S(2)}, u32[]{:S(2)}) collective-permute-start(bf16[32,2048]{1,0:T(8,128)(2,1)S(1)} %bitcast.18), channel_id=1, source_target_pairs={{0,224},{32,0},{64,32},{96,64},{128,96},{160,128},{192,160},{224,1... | collective-permute-start | bytes 393224 | tf_op jit(solution)/shard_map/ppermute | solution.py:34
  8.5 3.1 %collective-permute-done.3.rest_7_ = bf16[32,2048]{1,0:T(8,128)(2,1)S(1)} collective-permute-done((bf16[32,2048]{1,0:T(8,128)(2,1)S(1)}, bf16[32,2048]{1,0:T(8,128)(2,1)S(1)}, u32[]{:S(2)}, u32[]{:S(2)}) %collective-permute-start.3) | collective-permute-done | bytes 131104 | tf_op jit(solution)/shard_map/ppermute | solution.py:34
  21.2 3.4 %collective-permute-start.8 = (bf16[32,2048]{1,0:T(8,128)(2,1)S(1)}, bf16[32,2048]{1,0:T(8,128)(2,1)S(1)}, u32[]{:S(2)}, u32[]{:S(2)}) collective-permute-start(bf16[32,2048]{1,0:T(8,128)(2,1)S(1)} %collective-permute-done.7.rest_2_), channel_id=1, source_target_pairs={{0,224},{32,0},{64,32},{96,64},{128,96},{160,128},{192,160},{224,1... | collective-permute-start | bytes 393224 | tf_op jit(solution)/shard_map/ppermute | solution.py:34
  26.6 3.1 %collective-permute-start.10 = (bf16[128,2048]{1,0:T(8,128)(2,1)S(1)}, bf16[128,2048]{1,0:T(8,128)(2,1)S(1)}, u32[]{:S(2)}, u32[]{:S(2)}) collective-permute-start(bf16[128,2048]{1,0:T(8,128)(2,1)S(1)} %joined.2.rest_0_), channel_id=1, source_target_pairs={{0,224},{32,0},{64,32},{96,64},{128,96},{160,128},{192,160},{224,1... | collective-permute-start | bytes 1572872 | tf_op jit(solution)/shard_map/ppermute | solution.py:34
  33.4 3.1 %collective-permute-done.10.rest_2_ = bf16[128,2048]{1,0:T(8,128)(2,1)S(1)} collective-permute-done((bf16[128,2048]{1,0:T(8,128)(2,1)S(1)}, bf16[128,2048]{1,0:T(8,128)(2,1)S(1)}, u32[]{:S(2)}, u32[]{:S(2)}) %collective-permute-start.10) | collective-permute-done | bytes 524320 | tf_op jit(solution)/shard_map/ppermute | solution.py:34
  36.6 3.7 %collective-permute-done.9.rest_1_ = bf16[128,2048]{1,0:T(8,128)(2,1)S(1)} collective-permute-done((bf16[128,2048]{1,0:T(8,128)(2,1)S(1)}, bf16[128,2048]{1,0:T(8,128)(2,1)S(1)}, u32[]{:S(2)}, u32[]{:S(2)}) %collective-permute-start.9) | collective-permute-done | bytes 524320 | tf_op jit(solution)/shard_map/ppermute | solution.py:34
  40.3 2.7 %collective-permute-start.12 = (bf16[128,2048]{1,0:T(8,128)(2,1)S(1)}, bf16[128,2048]{1,0:T(8,128)(2,1)S(1)}, u32[]{:S(2)}, u32[]{:S(2)}) collective-permute-start(bf16[128,2048]{1,0:T(8,128)(2,1)S(1)} %collective-permute-done.10.rest_2_), channel_id=1, source_target_pairs={{0,224},{32,0},{64,32},{96,64},{128,96},{160,128},{192,160},{224,1... | collective-permute-start | bytes 1572872 | tf_op jit(solution)/shard_map/ppermute | solution.py:34
  43.6 7.1 %collective-permute-done.11.rest_3_ = bf16[128,2048]{1,0:T(8,128)(2,1)S(1)} collective-permute-done((bf16[128,2048]{1,0:T(8,128)(2,1)S(1)}, bf16[128,2048]{1,0:T(8,128)(2,1)S(1)}, u32[]{:S(2)}, u32[]{:S(2)}) %collective-permute-start.11) | collective-permute-done | bytes 524320 | tf_op jit(solution)/shard_map/ppermute | solution.py:34
  50.7 2.7 %collective-permute-start.14 = (bf16[128,2048]{1,0:T(8,128)(2,1)S(1)}, bf16[128,2048]{1,0:T(8,128)(2,1)S(1)}, u32[]{:S(2)}, u32[]{:S(2)}) collective-permute-start(bf16[128,2048]{1,0:T(8,128)(2,1)S(1)} %collective-permute-done.12.rest_4_), channel_id=1, source_target_pairs={{0,224},{32,0},{64,32},{96,64},{128,96},{160,128},{192,160},{224,1... | collective-permute-start | bytes 1572872 | tf_op jit(solution)/shard_map/ppermute | solution.py:34
  56.2 2.9 %early_scores.1 = (f32[640,512]{1,0:T(8,128)S(1)}, bf16[640,2048]{1,0:T(8,128)(2,1)S(1)}) custom-call(bf16[512,2048]{1,0:T(8,128)(2,1)S(1)} %bitcast.14, f32[1,2048]{1,0:T(1,128)S(1)} %bitcast.24, f32[1,512]{1,0:T(1,128)S(1)} %bitcast.27, bf16[128,2048]{1,0:T(8,128)(2,1)S(1)} %joined.2.rest_0_, bf16[128,2048]{1,0:T(8,128)(2,1)S(1)} %collective-permute-done.9.rest_1_, ...), custom_call_target="tpu_custom_call" | custom-call | flops 1342177280 | bytes 8388608 | tf_op jit(solution)/shard_map/early_scores/pallas_call | solution.py:166
  61.8 3.0 %collective-permute-start.16 = (bf16[64,2048]{1,0:T(8,128)(2,1)S(1)}, bf16[64,2048]{1,0:T(8,128)(2,1)S(1)}, u32[]{:S(2)}, u32[]{:S(2)}) collective-permute-start(bf16[64,2048]{1,0:T(8,128)(2,1)S(1)} %get-tuple-element.50), channel_id=1, source_target_pairs={{0,224},{32,0},{64,32},{96,64},{128,96},{160,128},{192,160},{224,1... | collective-permute-start | bytes 786440 | tf_op jit(solution)/shard_map/ppermute | solution.py:34
  64.8 5.4 %partial_scores.3 = (f32[384,512]{1,0:T(8,128)S(1)}, f32[192,512]{1,0:T(8,128)S(1)}, f32[192,512]{1,0:T(8,128)S(1)}, bf16[1024,2048]{1,0:T(8,128)(2,1)}) custom-call(s32[143]{0:T(256)S(1)} %compare_select_fusion.23.refs__0_.tab, bf16[512,2048]{1,0:T(8,128)(2,1)S(1)} %bitcast.15, f32[1,2048]{1,0:T(1,128)S(1)} %bitcast.25, f32[1,512]{1,0:T(1,128)S(1)} %bitcast.28, ...), custom_call_target="tpu_custom_call" | custom-call | flops 2147483648 | bytes 8388608 | tf_op jit(solution)/shard_map/partial_scores/pallas_call | solution.py:230
  70.3 2.8 %collective-permute-start.24 = (f32[384,512]{1,0:T(8,128)S(1)}, f32[384,512]{1,0:T(8,128)S(1)}, u32[]{:S(2)}, u32[]{:S(2)}) collective-permute-start(f32[384,512]{1,0:T(8,128)S(1)} %get-tuple-element.59), channel_id=1, source_target_pairs={{0,3},{3,0},{1,2},{2,1},{4,7},{7,4},{5,6},{6,5},{8,11},{11,8},{9,1... | collective-permute-start | bytes 2359304 | tf_op jit(solution)/shard_map/ppermute | solution.py:538
  73.1 3.5 %partial_scores.2 = (f32[384,512]{1,0:T(8,128)S(1)}, f32[192,512]{1,0:T(8,128)S(1)}, f32[192,512]{1,0:T(8,128)S(1)}, bf16[384,2048]{1,0:T(8,128)(2,1)S(1)}) custom-call(s32[143]{0:T(256)S(1)} %compare_select_fusion.23.refs__0_.tab, bf16[512,2048]{1,0:T(8,128)(2,1)S(1)} %bitcast.16, f32[1,2048]{1,0:T(1,128)S(1)} %bitcast.26, f32[1,512]{1,0:T(1,128)S(1)} %bitcast.29, ...), custom_call_target="tpu_custom_call" | custom-call | flops 805306368 | bytes 8388608 | tf_op jit(solution)/shard_map/partial_scores/pallas_call | solution.py:230
  76.7 5.8 %collective-permute-done.24.b1 = f32[384,512]{1,0:T(8,128)S(1)} collective-permute-done((f32[384,512]{1,0:T(8,128)S(1)}, f32[384,512]{1,0:T(8,128)S(1)}, u32[]{:S(2)}, u32[]{:S(2)}) %collective-permute-start.24) | collective-permute-done | bytes 786464 | tf_op jit(solution)/shard_map/ppermute | solution.py:538
  83.1 4.8 %collective-permute-done.17.a1 = f32[384,512]{1,0:T(8,128)S(1)} collective-permute-done((f32[384,512]{1,0:T(8,128)S(1)}, f32[384,512]{1,0:T(8,128)S(1)}, u32[]{:S(2)}, u32[]{:S(2)}) %collective-permute-start.17) | collective-permute-done | bytes 786464 | tf_op jit(solution)/shard_map/ppermute | solution.py:538
  89.1 4.1 %collective-permute-done.25.b2 = f32[192,512]{1,0:T(8,128)S(1)} collective-permute-done((f32[192,512]{1,0:T(8,128)S(1)}, f32[192,512]{1,0:T(8,128)S(1)}, u32[]{:S(2)}, u32[]{:S(2)}) %collective-permute-start.25) | collective-permute-done | bytes 393248 | tf_op jit(solution)/shard_map/ppermute | solution.py:539
  93.2 4.5 %collective-permute-done.18.a2 = f32[192,512]{1,0:T(8,128)S(1)} collective-permute-done((f32[192,512]{1,0:T(8,128)S(1)}, f32[192,512]{1,0:T(8,128)S(1)}, u32[]{:S(2)}, u32[]{:S(2)}) %collective-permute-start.18) | collective-permute-done | bytes 393248 | tf_op jit(solution)/shard_map/ppermute | solution.py:539
  102.4 7.5 %all-to-all-start = ((f32[32,8,128]{2,1,0:T(8,128)}), f32[32,8,128]{2,1,0:T(8,128)S(1)}, u32[]{:S(2)}, u32[]{:S(2)}) async-start(f32[32,8,128]{2,1,0:T(8,128)} %get-tuple-element.61.own), calls=%async_computation | async-start | bytes 262144 | tf_op jit(solution)/shard_map/all_to_all | solution.py:552
  115.6 3.6 %all-to-all-done.everyone = f32[32,8,128]{2,1,0:T(8,128)S(1)} async-done(((f32[32,8,128]{2,1,0:T(8,128)}), f32[32,8,128]{2,1,0:T(8,128)S(1)}, u32[]{:S(2)}, u32[]{:S(2)}) %all-to-all-start) | async-done | bytes 131104 | tf_op jit(solution)/shard_map/all_to_all | solution.py:552
  123.7 3.0 %lay_posteriors.1.rest_4_ = bf16[512,2048]{1,0:T(8,128)(2,1)S(1)} custom-call(s32[143]{0:T(256)S(1)} %compare_select_fusion.23.refs__0_.tab, bf16[384,512]{1,0:T(8,128)(2,1)} %get-tuple-element.62.own, bf16[384,512]{1,0:T(8,128)(2,1)S(1)} %collective-permute-done.29.first.far, bf16[384,512]{1,0:T(8,128)(2,1)S(1)} %collective-permute-done.30.second.near, ...), custom_call_target="tpu_custom_call" | custom-call | bytes 16777216 | tf_op jit(solution)/shard_map/lay_posteriors/pallas_call | solution.py:439
  128.9 4.7 %weighted_send.1 = (f32[256,2048]{1,0:T(8,128)S(1)}, f32[1,2048]{1,0:T(1,128)S(1)}) custom-call(s32[143]{0:T(256)S(1)} %compare_select_fusion.23.refs__0_.tab, f32[8,128]{1,0:T(8,128)S(1)} %combine_stats.1.rest_0_, f32[8,128]{1,0:T(8,128)S(1)} %collective-permute-done.26.rest_1_, f32[8,128]{1,0:T(8,128)S(1)} %collective-permute-done.27.rest_2_, ...), custom_call_target="tpu_custom_call" | custom-call | flops 2147483648 | bytes 12582912 | tf_op jit(solution)/shard_map/weighted_send/pallas_call | solution.py:454
  133.6 17.1 %collective-permute-start.33 = (f32[256,2048]{1,0:T(8,128)S(1)}, f32[256,2048]{1,0:T(8,128)S(1)}, u32[]{:S(2)}, u32[]{:S(2)}) collective-permute-start(f32[256,2048]{1,0:T(8,128)S(1)} %get-tuple-element.70), channel_id=1, source_target_pairs={{0,4},{4,0},{1,5},{5,1},{2,6},{6,2},{3,7},{7,3},{8,12},{12,8},{9,1... | collective-permute-start | bytes 6291464 | tf_op jit(solution)/shard_map/ppermute | solution.py:470
  150.8 3.9 %weighted_keep.1 = (f32[256,2048]{1,0:T(8,128)S(1)}, f32[1,64]{1,0:T(1,128)}) custom-call(s32[143]{0:T(256)S(1)} %compare_select_fusion.23.refs__0_.tab, f32[8,128]{1,0:T(8,128)S(1)} %combine_stats.1.rest_0_, f32[8,128]{1,0:T(8,128)S(1)} %collective-permute-done.26.rest_1_, f32[8,128]{1,0:T(8,128)S(1)} %collective-permute-done.27.rest_2_, ...), custom_call_target="tpu_custom_call" | custom-call | flops 2147483648 | bytes 12582912 | tf_op jit(solution)/shard_map/weighted_keep/pallas_call | solution.py:471
  (88 shorter events, 46.2 us)
Async XLA Ops:
  4.5 12.1 %collective-permute-start.6 = (bf16[32,2048]{1,0:T(8,128)(2,1)S(1)}, bf16[32,2048]{1,0:T(8,128)(2,1)S(1)}, u32[]{:S(2)}, u32[]{:S(2)}) collective-permute-start(bf16[32,2048]{1,0:T(8,128)(2,1)S(1)} %bitcast.18), channel_id=1, source_target_pairs={{0,224},{32,0},{64,32},{96,64},{128,96},{160,128},{192,160},{224,1... | collective-permute-start | bytes 393224 | tf_op jit(solution)/shard_map/ppermute | solution.py:34
  11.7 12.9 %collective-permute-start.2 = (bf16[32,2048]{1,0:T(8,128)(2,1)S(1)}, bf16[32,2048]{1,0:T(8,128)(2,1)S(1)}, u32[]{:S(2)}, u32[]{:S(2)}) collective-permute-start(bf16[32,2048]{1,0:T(8,128)(2,1)S(1)} %bitcast.20), channel_id=1, source_target_pairs={{0,8},{8,16},{16,24},{24,0},{1,9},{9,17},{17,25},{25,1},{2,10},{10... | collective-permute-start | bytes 393224 | tf_op jit(solution)/shard_map/ppermute | solution.py:34
  13.0 11.6 %collective-permute-start.1 = (bf16[32,2048]{1,0:T(8,128)(2,1)S(1)}, bf16[32,2048]{1,0:T(8,128)(2,1)S(1)}, u32[]{:S(2)}, u32[]{:S(2)}) collective-permute-start(bf16[32,2048]{1,0:T(8,128)(2,1)S(1)} %bitcast.21), channel_id=1, source_target_pairs={{0,16},{8,24},{16,0},{24,8},{1,17},{9,25},{17,1},{25,9},{2,18},{10... | collective-permute-start | bytes 393224 | tf_op jit(solution)/shard_map/ppermute | solution.py:34
  26.6 10.0 %collective-permute-start.10 = (bf16[128,2048]{1,0:T(8,128)(2,1)S(1)}, bf16[128,2048]{1,0:T(8,128)(2,1)S(1)}, u32[]{:S(2)}, u32[]{:S(2)}) collective-permute-start(bf16[128,2048]{1,0:T(8,128)(2,1)S(1)} %joined.2.rest_0_), channel_id=1, source_target_pairs={{0,224},{32,0},{64,32},{96,64},{128,96},{160,128},{192,160},{224,1... | collective-permute-start | bytes 1572872 | tf_op jit(solution)/shard_map/ppermute | solution.py:34
  29.6 10.6 %collective-permute-start.9 = (bf16[128,2048]{1,0:T(8,128)(2,1)S(1)}, bf16[128,2048]{1,0:T(8,128)(2,1)S(1)}, u32[]{:S(2)}, u32[]{:S(2)}) collective-permute-start(bf16[128,2048]{1,0:T(8,128)(2,1)S(1)} %joined.2.rest_0_), channel_id=1, source_target_pairs={{0,32},{32,64},{64,96},{96,128},{128,160},{160,192},{192,224},{224... | collective-permute-start | bytes 1572872 | tf_op jit(solution)/shard_map/ppermute | solution.py:34
  31.1 22.3 %collective-permute-start.21 = (bf16[256,2048]{1,0:T(8,128)(2,1)S(1)}, bf16[256,2048]{1,0:T(8,128)(2,1)S(1)}, u32[]{:S(2)}, u32[]{:S(2)}) collective-permute-start(bf16[256,2048]{1,0:T(8,128)(2,1)S(1)} %joined.3.refs__4_), channel_id=1, source_target_pairs={{0,24},{8,0},{16,8},{24,16},{1,25},{9,1},{17,9},{25,17},{2,26},{10... | collective-permute-start | bytes 3145736 | tf_op jit(solution)/shard_map/ppermute | solution.py:34
  31.2 22.3 %collective-permute-start.20 = (bf16[256,2048]{1,0:T(8,128)(2,1)S(1)}, bf16[256,2048]{1,0:T(8,128)(2,1)S(1)}, u32[]{:S(2)}, u32[]{:S(2)}) collective-permute-start(bf16[256,2048]{1,0:T(8,128)(2,1)S(1)} %joined.3.refs__4_), channel_id=1, source_target_pairs={{0,8},{8,16},{16,24},{24,0},{1,9},{9,17},{17,25},{25,1},{2,10},{10... | collective-permute-start | bytes 3145736 | tf_op jit(solution)/shard_map/ppermute | solution.py:34
  40.3 10.5 %collective-permute-start.11 = (bf16[128,2048]{1,0:T(8,128)(2,1)S(1)}, bf16[128,2048]{1,0:T(8,128)(2,1)S(1)}, u32[]{:S(2)}, u32[]{:S(2)}) collective-permute-start(bf16[128,2048]{1,0:T(8,128)(2,1)S(1)} %collective-permute-done.9.rest_1_), channel_id=1, source_target_pairs={{0,32},{32,64},{64,96},{96,128},{128,160},{160,192},{192,224},{224... | collective-permute-start | bytes 1572872 | tf_op jit(solution)/shard_map/ppermute | solution.py:34
  40.3 10.5 %collective-permute-start.12 = (bf16[128,2048]{1,0:T(8,128)(2,1)S(1)}, bf16[128,2048]{1,0:T(8,128)(2,1)S(1)}, u32[]{:S(2)}, u32[]{:S(2)}) collective-permute-start(bf16[128,2048]{1,0:T(8,128)(2,1)S(1)} %collective-permute-done.10.rest_2_), channel_id=1, source_target_pairs={{0,224},{32,0},{64,32},{96,64},{128,96},{160,128},{192,160},{224,1... | collective-permute-start | bytes 1572872 | tf_op jit(solution)/shard_map/ppermute | solution.py:34
  50.7 10.9 %collective-permute-start.13 = (bf16[128,2048]{1,0:T(8,128)(2,1)S(1)}, bf16[128,2048]{1,0:T(8,128)(2,1)S(1)}, u32[]{:S(2)}, u32[]{:S(2)}) collective-permute-start(bf16[128,2048]{1,0:T(8,128)(2,1)S(1)} %collective-permute-done.11.rest_3_), channel_id=1, source_target_pairs={{0,32},{32,64},{64,96},{96,128},{128,160},{160,192},{192,224},{224... | collective-permute-start | bytes 1572872 | tf_op jit(solution)/shard_map/ppermute | solution.py:34
  50.7 10.9 %collective-permute-start.14 = (bf16[128,2048]{1,0:T(8,128)(2,1)S(1)}, bf16[128,2048]{1,0:T(8,128)(2,1)S(1)}, u32[]{:S(2)}, u32[]{:S(2)}) collective-permute-start(bf16[128,2048]{1,0:T(8,128)(2,1)S(1)} %collective-permute-done.12.rest_4_), channel_id=1, source_target_pairs={{0,224},{32,0},{64,32},{96,64},{128,96},{160,128},{192,160},{224,1... | collective-permute-start | bytes 1572872 | tf_op jit(solution)/shard_map/ppermute | solution.py:34
  53.5 11.4 %collective-permute-start.22 = (bf16[128,2048]{1,0:T(8,128)(2,1)S(1)}, bf16[128,2048]{1,0:T(8,128)(2,1)S(1)}, u32[]{:S(2)}, u32[]{:S(2)}) collective-permute-start(bf16[128,2048]{1,0:T(8,128)(2,1)S(1)} %get-tuple-element.56), channel_id=1, source_target_pairs={{0,8},{8,16},{16,24},{24,0},{1,9},{9,17},{17,25},{25,1},{2,10},{10... | collective-permute-start | bytes 1572872 | tf_op jit(solution)/shard_map/ppermute | solution.py:34
  53.6 11.3 %collective-permute-start.23 = (bf16[128,2048]{1,0:T(8,128)(2,1)S(1)}, bf16[128,2048]{1,0:T(8,128)(2,1)S(1)}, u32[]{:S(2)}, u32[]{:S(2)}) collective-permute-start(bf16[128,2048]{1,0:T(8,128)(2,1)S(1)} %get-tuple-element.57), channel_id=1, source_target_pairs={{0,24},{8,0},{16,8},{24,16},{1,25},{9,1},{17,9},{25,17},{2,26},{10... | collective-permute-start | bytes 1572872 | tf_op jit(solution)/shard_map/ppermute | solution.py:34
  61.7 11.4 %collective-permute-start.15 = (bf16[64,2048]{1,0:T(8,128)(2,1)S(1)}, bf16[64,2048]{1,0:T(8,128)(2,1)S(1)}, u32[]{:S(2)}, u32[]{:S(2)}) collective-permute-start(bf16[64,2048]{1,0:T(8,128)(2,1)S(1)} %get-tuple-element.49), channel_id=1, source_target_pairs={{0,32},{32,64},{64,96},{96,128},{128,160},{160,192},{192,224},{224... | collective-permute-start | bytes 786440 | tf_op jit(solution)/shard_map/ppermute | solution.py:34
  61.8 11.3 %collective-permute-start.16 = (bf16[64,2048]{1,0:T(8,128)(2,1)S(1)}, bf16[64,2048]{1,0:T(8,128)(2,1)S(1)}, u32[]{:S(2)}, u32[]{:S(2)}) collective-permute-start(bf16[64,2048]{1,0:T(8,128)(2,1)S(1)} %get-tuple-element.50), channel_id=1, source_target_pairs={{0,224},{32,0},{64,32},{96,64},{128,96},{160,128},{192,160},{224,1... | collective-permute-start | bytes 786440 | tf_op jit(solution)/shard_map/ppermute | solution.py:34
  70.3 12.2 %collective-permute-start.24 = (f32[384,512]{1,0:T(8,128)S(1)}, f32[384,512]{1,0:T(8,128)S(1)}, u32[]{:S(2)}, u32[]{:S(2)}) collective-permute-start(f32[384,512]{1,0:T(8,128)S(1)} %get-tuple-element.59), channel_id=1, source_target_pairs={{0,3},{3,0},{1,2},{2,1},{4,7},{7,4},{5,6},{6,5},{8,11},{11,8},{9,1... | collective-permute-start | bytes 2359304 | tf_op jit(solution)/shard_map/ppermute | solution.py:538
  76.6 11.2 %collective-permute-start.17 = (f32[384,512]{1,0:T(8,128)S(1)}, f32[384,512]{1,0:T(8,128)S(1)}, u32[]{:S(2)}, u32[]{:S(2)}) collective-permute-start(f32[384,512]{1,0:T(8,128)S(1)} %get-tuple-element.52), channel_id=1, source_target_pairs={{0,1},{1,0},{2,3},{3,2},{4,5},{5,4},{6,7},{7,6},{8,9},{9,8},{10,11... | collective-permute-start | bytes 2359304 | tf_op jit(solution)/shard_map/ppermute | solution.py:538
  82.6 10.6 %collective-permute-start.25 = (f32[192,512]{1,0:T(8,128)S(1)}, f32[192,512]{1,0:T(8,128)S(1)}, u32[]{:S(2)}, u32[]{:S(2)}) collective-permute-start(f32[192,512]{1,0:T(8,128)S(1)} %slice_add_fusion), channel_id=1, source_target_pairs={{0,1},{1,0},{2,3},{3,2},{4,5},{5,4},{6,7},{7,6},{8,9},{9,8},{10,11... | collective-permute-start | bytes 1179656 | tf_op jit(solution)/shard_map/ppermute | solution.py:539
  99.6 10.3 %collective-permute-start.30 = (bf16[384,512]{1,0:T(8,128)(2,1)}, bf16[384,512]{1,0:T(8,128)(2,1)S(1)}, u32[]{:S(2)}, u32[]{:S(2)}) collective-permute-start(bf16[384,512]{1,0:T(8,128)(2,1)} %get-tuple-element.62.own), channel_id=1, source_target_pairs={{0,1},{1,0},{2,3},{3,2},{4,5},{5,4},{6,7},{7,6},{8,9},{9,8},{10,11... | collective-permute-start | bytes 1179656 | tf_op jit(solution)/shard_map/ppermute | solution.py:547
  100.0 11.6 %collective-permute-start.29 = (bf16[384,512]{1,0:T(8,128)(2,1)}, bf16[384,512]{1,0:T(8,128)(2,1)S(1)}, u32[]{:S(2)}, u32[]{:S(2)}) collective-permute-start(bf16[384,512]{1,0:T(8,128)(2,1)} %get-tuple-element.62.own), channel_id=1, source_target_pairs={{0,3},{3,0},{1,2},{2,1},{4,7},{7,4},{5,6},{6,5},{8,11},{11,8},{9,1... | collective-permute-start | bytes 1179656 | tf_op jit(solution)/shard_map/ppermute | solution.py:548
  102.4 16.8 %all-to-all-start = ((f32[32,8,128]{2,1,0:T(8,128)}), f32[32,8,128]{2,1,0:T(8,128)S(1)}, u32[]{:S(2)}, u32[]{:S(2)}) async-start(f32[32,8,128]{2,1,0:T(8,128)} %get-tuple-element.61.own), calls=%async_computation | async-start | bytes 262144 | tf_op jit(solution)/shard_map/all_to_all | solution.py:552
  112.4 11.2 %collective-permute-start.31 = (bf16[192,512]{1,0:T(8,128)(2,1)}, bf16[192,512]{1,0:T(8,128)(2,1)}, u32[]{:S(2)}, u32[]{:S(2)}) collective-permute-start(bf16[192,512]{1,0:T(8,128)(2,1)} %get-tuple-element.63), channel_id=1, source_target_pairs={{0,1},{1,0},{2,3},{3,2},{4,5},{5,4},{6,7},{7,6},{8,9},{9,8},{10,11... | collective-permute-start | bytes 589832 | tf_op jit(solution)/shard_map/ppermute | solution.py:550
  113.1 10.5 %collective-permute-start.32 = (bf16[192,512]{1,0:T(8,128)(2,1)}, bf16[192,512]{1,0:T(8,128)(2,1)}, u32[]{:S(2)}, u32[]{:S(2)}) collective-permute-start(bf16[192,512]{1,0:T(8,128)(2,1)} %get-tuple-element.64), channel_id=1, source_target_pairs={{0,3},{3,0},{1,2},{2,1},{4,7},{7,4},{5,6},{6,5},{8,11},{11,8},{9,1... | collective-permute-start | bytes 589832 | tf_op jit(solution)/shard_map/ppermute | solution.py:551
  133.6 21.0 %collective-permute-start.33 = (f32[256,2048]{1,0:T(8,128)S(1)}, f32[256,2048]{1,0:T(8,128)S(1)}, u32[]{:S(2)}, u32[]{:S(2)}) collective-permute-start(f32[256,2048]{1,0:T(8,128)S(1)} %get-tuple-element.70), channel_id=1, source_target_pairs={{0,4},{4,0},{1,5},{5,1},{2,6},{6,2},{3,7},{7,3},{8,12},{12,8},{9,1... | collective-permute-start | bytes 6291464 | tf_op jit(solution)/shard_map/ppermute | solution.py:470
  (18 other events, 160.5 us)
